TPU v7x, 256 devices: a whole 4x4x8 slice. The times are simulated.
256 devices in a mesh: ia: 16 (over z, y_lo), ja: 4 (over y_hi, core), ka: 4 (over x).
Axes of the slice: x: 4, y: 4 (y_hi: 2, y_lo: 2; y = y_hi * 2 + y_lo), z: 8, core: 2. Of those that a mesh axis runs over, the one named last changes fastest.
Arguments:
- tensor: float32 [96, 2048, 2048], P('ka', 'ia', 'ja'), may hold values from -6 to 6
- factor_b: float32 [2048, 256], P(('ja', 'ia', 'ka')), as said below
- factor_c: float32 [96, 256], P('ka'), as said below
Outputs:
- hat_a: float32 [2048, 256], P(('ia', 'ja', 'ka'))
- weight_a: float32 [256], replicated
- hat_b: float32 [2048, 256], P(('ja', 'ia', 'ka'))
- weight_b: float32 [256], replicated
Inputs may be any that keep to these rules, and one draw needn't show every extreme that they name: `factor_b`: Real-valued factor entries; entries of one row may be correlated. `factor_c`: Real-valued factor entries; entries of one row may be correlated.
All inputs are finite; a program needn't handle non-finite values.
Results may differ from a plain program's by a relative error of at most 0.00018.
Values sent between devices are 32-bit elements; how exact they have to be, the bound alone decides.
A program may use at most 64 MiB of HBM per device.

v0:
```python
import jax
import jax.numpy as jnp
from jax import lax
from jax.sharding import PartitionSpec as P

ridge_term = 0.01
epsilon = 1e-06


def solve_rows(system, right):
    lower = jnp.linalg.cholesky(system)
    return jax.scipy.linalg.cho_solve((lower, True), right.T).T


def local(tensor, factor_b, factor_c):
    high = lax.Precision.HIGHEST
    depth, height, width = tensor.shape
    rank = factor_c.shape[1]
    identity = jnp.eye(rank, dtype=jnp.float32)
    total_a = height * lax.axis_size("ia")
    total_b = width * lax.axis_size("ja")
    gram_c = lax.psum(
        jnp.dot(factor_c.T, factor_c, precision=high, preferred_element_type=jnp.float32), "ka"
    )
    gram_b = lax.psum(
        jnp.dot(factor_b.T, factor_b, precision=high, preferred_element_type=jnp.float32),
        ("ia", "ja", "ka"),
    )
    flat = tensor.reshape(depth * height, width)
    along_j = jnp.dot(
        flat,
        lax.all_gather(factor_b, ("ia", "ka"), axis=0, tiled=True),
        precision=high,
        preferred_element_type=jnp.float32,
    )
    partial_a = jnp.sum(along_j.reshape(depth, height, rank) * factor_c[:, None, :], axis=0)
    system_a = gram_b * gram_c + ridge_term * identity
    share_a = lax.psum_scatter(partial_a, ("ja", "ka"), scatter_dimension=0, tiled=True)
    raw_a = solve_rows(system_a, share_a)
    squares_a = lax.psum(jnp.sum(raw_a * raw_a, axis=0), ("ia", "ja", "ka"))
    weight_a = jnp.sqrt(squares_a / total_a + epsilon)
    hat_a = raw_a / weight_a
    gram_a = lax.psum(
        jnp.dot(hat_a.T, hat_a, precision=high, preferred_element_type=jnp.float32),
        ("ia", "ja", "ka"),
    )
    along_i = jnp.einsum(
        "kij,ir->kjr",
        tensor,
        lax.all_gather(hat_a, ("ja", "ka"), axis=0, tiled=True),
        precision=high,
        preferred_element_type=jnp.float32,
    )
    partial_b = jnp.sum(along_i * factor_c[:, None, :], axis=0)
    share_b = lax.psum_scatter(partial_b, ("ia", "ka"), scatter_dimension=0, tiled=True)
    raw_b = solve_rows(gram_a * gram_c + ridge_term * identity, share_b)
    squares_b = lax.psum(jnp.sum(raw_b * raw_b, axis=0), ("ia", "ja", "ka"))
    weight_b = jnp.sqrt(squares_b / total_b + epsilon)
    hat_b = raw_b / weight_b
    return (hat_a, weight_a, hat_b, weight_b)


def solution(mesh):
    return jax.shard_map(
        local,
        mesh=mesh,
        in_specs=(P("ka", "ia", "ja"), P(("ja", "ia", "ka"), None), P("ka", None)),
        out_specs=(P(("ia", "ja", "ka"), None), P(), P(("ja", "ia", "ka"), None), P()),
        check_vma=False,
    )
```

profile of v0, /device:TPU:1, one launch (start us, length us, event | category | flops | bytes accessed | tf_op | source)
XLA Modules:
  0.0 900.2 jit_solution(3671649565068929056)
XLA Ops:
  8.0 1.9 fusion.32
  10.0 1.9 fusion.33
  12.0 134.7 %all_gather.6 = f32[512,256]{1,0:T(8,128)S(1)} all-gather(f32[8,256]{1,0:T(8,128)} %param.7), channel_id=1, replica_groups=mesh['ia'=16,'ja'=4,'ka'=4] {'ia','ka'}, dimensions={0}, use_global_device_ids=true | all-gather | bytes 532480 | tf_op jit(solution)/shard_map/all_gather | solution.py:32
  146.7 8.5 multiply_reduce_fusion
  155.6 111.5 %all-reduce.5.cloned.1.call-done = f32[256,256]{0,1:T(8,128)} async-done(((f32[256,256]{0,1:T(8,128)}), f32[256,256]{0,1:T(8,128)}) %all-reduce.5.cloned.1.call-update) | async-done | bytes 262160 | tf_op jit(solution)/shard_map/psum | solution.py:25
  267.1 47.3 %all-reduce.7.cloned.1.call-done = f32[256,256]{0,1:T(8,128)} async-done(((f32[256,256]{0,1:T(8,128)}), f32[256,256]{0,1:T(8,128)}) %all-reduce.7.cloned.1.call-update) | async-done | bytes 262160 | tf_op jit(solution)/shard_map/psum | solution.py:22
  315.7 11.7 %cholesky.130 = f32[128,128]{1,0:T(8,128)S(1)} custom-call(f32[128,128]{1,0:T(8,128)S(1)} %cholesky.194), custom_call_target="Cholesky" | custom-call | tf_op jit(solution)/shard_map/jit(cholesky)/cholesky | solution.py:11
  327.4 9.8 %custom-call.15 = f32[1,128,128]{1,2,0:T(8,128)S(1)} custom-call(f32[1,128,128]{2,1,0:T(8,128)S(1)} %get-tuple-element.49), custom_call_target="InvertDiagBlocksLowerTriangular" | custom-call | tf_op jit(solution)/shard_map/jit(cholesky)/cholesky | solution.py:11
  337.7 11.7 %cholesky.147 = f32[128,128]{1,0:T(8,128)S(1)} custom-call(f32[128,128]{1,0:T(8,128)S(1)} %convolution_subtract_fusion.1), custom_call_target="Cholesky" | custom-call | tf_op jit(solution)/shard_map/jit(cholesky)/cholesky | solution.py:11
  351.5 4.5 while.4
  354.7 1.4 bitcast_dynamic-update-slice_fusion.4
  356.1 19.7 %custom-call.16 = f32[2,128,128]{1,2,0:T(8,128)S(1)} custom-call(f32[2,128,128]{2,1,0:T(8,128)S(1)} %get-tuple-element.20), custom_call_target="InvertDiagBlocksLowerTriangular" | custom-call | tf_op jit(solution)/shard_map/jit(_cho_solve)/triangular_solve | solution.py:12
  378.4 78.0 %psum.37 = f32[256]{0:T(256)S(1)} all-reduce(f32[256]{0:T(256)S(1)} %multiply_reduce_fusion.2), channel_id=1, replica_groups=mesh['ia'=16,'ja'=4,'ka'=4] {'ia','ja','ka'}, use_global_device_ids=true, to_apply=%region_9.0 | all-reduce | flops 256 | bytes 2048 | tf_op jit(solution)/shard_map/psum | solution.py:40
  457.5 28.9 %all_gather.7 = f32[128,256]{1,0:T(8,128)S(1)} all-gather(f32[8,256]{1,0:T(8,128)S(1)} %fusion.28), channel_id=1, replica_groups=mesh['ia'=16,'ja'=4,'ka'=4] {'ja','ka'}, dimensions={0}, use_global_device_ids=true | all-gather | bytes 139264 | tf_op jit(solution)/shard_map/all_gather | solution.py:50
  486.6 13.0 %fusion = f32[512,256]{0,1:T(8,128)S(1)} fusion(f32[24,256]{1,0:T(8,128)S(1)} %copy-done.1, f32[24,128,512]{2,1,0:T(8,128)} %param.6, f32[128,256]{1,0:T(8,128)S(1)} %all_gather.7), kind=kOutput, calls=%fused_computation.5 | convolution fusion | flops 4837998592 | bytes 6971392 | tf_op jit(solution)/shard_map/kij,ir->kjr/dot_general | solution.py:47
  500.6 237.9 %all-reduce.9.cloned.1.call-done = f32[256,256]{0,1:T(8,128)} async-done(((f32[256,256]{0,1:T(8,128)}), f32[256,256]{0,1:T(8,128)}) %all-reduce.9.cloned.1.call-update) | async-done | bytes 262160 | tf_op jit(solution)/shard_map/psum | solution.py:43
  739.7 11.7 %cholesky.164 = f32[128,128]{1,0:T(8,128)S(1)} custom-call(f32[128,128]{1,0:T(8,128)S(1)} %cholesky.197), custom_call_target="Cholesky" | custom-call | tf_op jit(solution)/shard_map/jit(cholesky)/cholesky | solution.py:11
  751.4 9.8 %custom-call.17 = f32[1,128,128]{1,2,0:T(8,128)S(1)} custom-call(f32[1,128,128]{2,1,0:T(8,128)S(1)} %get-tuple-element.45), custom_call_target="InvertDiagBlocksLowerTriangular" | custom-call | tf_op jit(solution)/shard_map/jit(cholesky)/cholesky | solution.py:11
  761.8 11.7 %cholesky.181 = f32[128,128]{1,0:T(8,128)S(1)} custom-call(f32[128,128]{1,0:T(8,128)S(1)} %convolution_subtract_fusion), custom_call_target="Cholesky" | custom-call | tf_op jit(solution)/shard_map/jit(cholesky)/cholesky | solution.py:11
  776.3 4.1 while.5
  776.9 1.4 bitcast_dynamic-update-slice_fusion.5
  778.9 1.4 bitcast_dynamic-update-slice_fusion.5
  780.4 19.9 %custom-call.18 = f32[2,128,128]{1,2,0:T(8,128)S(1)} custom-call(f32[2,128,128]{2,1,0:T(8,128)S(1)} %get-tuple-element.21), custom_call_target="InvertDiagBlocksLowerTriangular" | custom-call | tf_op jit(solution)/shard_map/jit(_cho_solve)/triangular_solve | solution.py:12
  802.9 89.4 %psum.39 = f32[256]{0:T(256)S(1)} all-reduce(f32[256]{0:T(256)S(1)} %multiply_reduce_fusion.1), channel_id=1, replica_groups=mesh['ia'=16,'ja'=4,'ka'=4] {'ia','ja','ka'}, use_global_device_ids=true, to_apply=%region_14.17 | all-reduce | flops 256 | bytes 2048 | tf_op jit(solution)/shard_map/psum | solution.py:57
  (78 shorter events, 18.0 us)
Async XLA Ops:
  8.0 259.1 %all-reduce.5.cloned.1.call-start = ((), (), s32[]{:S(2)}) async-start(), calls=%async_computation.2 | async-start | bytes 524288 | tf_op jit(solution)/shard_map/psum | solution.py:25
  10.0 304.4 %all-reduce.7.cloned.1.call-start = ((), (), s32[]{:S(2)}) async-start(), calls=%async_computation.3 | async-start | bytes 524288 | tf_op jit(solution)/shard_map/psum | solution.py:22
  12.0 363.8 %reduce-scatter.5.cloned.1.call-start = ((), (), s32[]{:S(2)}) async-start(), calls=%async_computation.4 | async-start | bytes 139264 | tf_op jit(solution)/shard_map/reduce_scatter | solution.py:38
  146.7 339.9 %copy-start.1 = (f32[24,256]{1,0:T(8,128)S(1)}, f32[24,256]{1,0:T(8,128)}, u32[]{:S(2)}) copy-start(f32[24,256]{1,0:T(8,128)} %param.8) | copy-start | bytes 73732
  155.2 583.3 %all-reduce.9.cloned.1.call-start = ((), (), s32[]{:S(2)}) async-start(), calls=%async_computation.5 | async-start | bytes 524288 | tf_op jit(solution)/shard_map/psum | solution.py:43
  315.6 422.9 %copy-start = (f32[256,256]{0,1:T(8,128)S(1)}, f32[256,256]{0,1:T(8,128)}, u32[]{:S(2)}) copy-start(f32[256,256]{0,1:T(8,128)} %all-reduce.7.cloned.1.call-done) | copy-start | bytes 786436
  456.4 317.1 %copy-start.3 = (f32[256]{0:T(256)}, f32[256]{0:T(256)S(1)}, u32[]{:S(2)}) copy-start(f32[256]{0:T(256)S(1)} %add_sqrt_fusion.1) | copy-start | bytes 3076
  456.4 317.8 %copy-start.2 = (f32[8,256]{1,0:T(8,128)}, f32[8,256]{1,0:T(8,128)S(1)}, u32[]{:S(2)}) copy-start(f32[8,256]{1,0:T(8,128)S(1)} %fusion.28) | copy-start | bytes 24580
  486.5 313.8 %reduce-scatter.7.cloned.1.call-start = ((), (), s32[]{:S(2)}) async-start(), calls=%async_computation.6 | async-start | bytes 532480 | tf_op jit(solution)/shard_map/reduce_scatter | solution.py:55
  892.3 0.6 copy-start.4
Sparse Core Ops, SparseCore 0:
  14.3 252.7 all-reduce.4
  269.4 44.9 all-reduce.6
  486.6 251.8 all-reduce.8
Sparse Core Ops, SparseCore 1:
  155.3 93.3 reduce-scatter.4
  500.6 264.4 reduce-scatter.6
where the time goes:
time: 904 us; the launch traced here: 900 us
  waiting for transfers between devices  397 us (44%)
  blocking collectives  331 us (37%)
  other arithmetic  111 us (12%)
  matrix products  32.4 us (4%)
  between operations  18.3 us (2%)
  local copies, waits for them, and re-layouts  9.42 us (1%)
    psum x1, waiting for transfers between devices, local(): lax.psum(jnp.dot(hat_a.T, hat_a, precision=high, preferred_element_type=j...  238 us
    all_gather x1, blocking collectives, local(): lax.all_gather(factor_b, ('ia', 'ka'), axis=0, tiled=True)  135 us
    psum x1, waiting for transfers between devices, local(): lax.psum(jnp.dot(factor_b.T, factor_b, precision=high, preferred_element_...  112 us
    psum x1, blocking collectives, local(): squares_b = lax.psum(jnp.sum(raw_b * raw_b, axis=0), ('ia', 'ja', 'ka'))  89.4 us
    psum x1, blocking collectives, local(): squares_a = lax.psum(jnp.sum(raw_a * raw_a, axis=0), ('ia', 'ja', 'ka'))  78 us
    another operation x13, other arithmetic, solve_rows(): lower = jnp.linalg.cholesky(system)  68.6 us
    psum x1, waiting for transfers between devices, local(): lax.psum(jnp.dot(factor_c.T, factor_c, precision=high, preferred_element_...  47.3 us
    another operation x5, other arithmetic, solve_rows(): return jax.scipy.linalg.cho_solve((lower, True), right.T).T  39.6 us
  transfers between devices with their start and end apart: 5, of which 3 were waited for; matrix products, arithmetic and copies ran while one was open for 16% of the time, Pallas kernels for 0%

commit v1 on v0

v1 whole, which is shorter than its diff:
```python
import functools

import jax
import jax.numpy as jnp
from jax import lax
from jax.experimental import pallas as pl
from jax.experimental.pallas import tpu as pltpu
from jax.sharding import PartitionSpec as P

ridge_term = 0.01
epsilon = 1e-06

MESH = pl.DeviceIdType.MESH
HIGH = lax.Precision.HIGHEST
F32 = jnp.float32
BF16 = jnp.bfloat16
NB = 16
TN = (((0,), (0,)), ((), ()))


def split2(x):
    hi = x.astype(BF16)
    return hi, (x - hi.astype(F32)).astype(BF16)


def split3(x):
    hi = x.astype(BF16)
    rest = x - hi.astype(F32)
    mid = rest.astype(BF16)
    return hi, mid, (rest - mid.astype(F32)).astype(BF16)


def sweep_panels(a_ref, first, last):
    rank = a_ref.shape[0]
    lane = lax.broadcasted_iota(jnp.int32, (NB, rank), 1)
    row = lax.broadcasted_iota(jnp.int32, (NB, rank), 0)
    row1 = lax.broadcasted_iota(jnp.int32, (NB, 128), 0)
    lane_all = lax.broadcasted_iota(jnp.int32, (rank, rank), 1)

    def wide(v):
        return jnp.concatenate([v] * (rank // 128), axis=1)

    def panel(b, carry):
        r0 = pl.multiple_of(b * NB, NB)
        r = a_ref[pl.ds(r0, NB), :]
        base = pl.multiple_of(lax.div(r0, 128) * 128, 128)
        half = a_ref[pl.ds(r0, NB), pl.ds(base, 128)]
        d = pltpu.roll(half, lax.rem(128 - (r0 - base), 128), 1)
        cols = [jnp.broadcast_to(d[:, j : j + 1], (NB, 128)) for j in range(NB)]
        inside = (lane >= r0) & (lane < r0 + NB)
        rz = jnp.where(inside, 0.0, r)
        q = jnp.where(inside, jnp.where(lane - r0 == row, -1.0, 0.0), r)
        for p in range(0, NB, 2):
            cp, cq = cols[p], cols[p + 1]
            a, b1, e = cp[p : p + 1], cp[p + 1 : p + 2], cq[p + 1 : p + 2]
            inv = 1.0 / (a * e - b1 * b1)
            fa, fb, fe = a * inv, b1 * inv, e * inv

            def apply(y, ma, mb, me, mp, mq, rows):
                yp, yq = y[p : p + 1], y[p + 1 : p + 2]
                np_ = me * yp - mb * yq
                nq_ = ma * yq - mb * yp
                new = y - mp * np_ - mq * nq_
                return jnp.where(rows == p, np_, jnp.where(rows == p + 1, nq_, new))

            for j in range(p + 2, NB):
                cols[j] = apply(cols[j], fa, fb, fe, cp, cq, row1)
            q = apply(q, wide(fa), wide(fb), wide(fe), wide(cp), wide(cq), row)
        r1, r2, r3 = split3(rz)
        q1, q2, q3 = split3(q)
        left = jnp.concatenate([r1, r1, r2, r2, r1, r3], axis=0)
        right = jnp.concatenate([q1, q2, q1, q2, q3, q1], axis=0)
        update = lax.dot_general(left, right, TN, preferred_element_type=F32)
        a_ref[...] = jnp.where((lane_all >= r0) & (lane_all < r0 + NB), 0.0, a_ref[...]) - update
        a_ref[pl.ds(r0, NB), :] = q
        return carry

    lax.fori_loop(first, last, panel, 0)


def diagonal(matrix):
    rank = matrix.shape[0]
    eye = lax.broadcasted_iota(jnp.int32, (rank, rank), 0) == lax.broadcasted_iota(jnp.int32, (rank, rank), 1)
    kept = jnp.where(eye, matrix, 0.0)
    return jnp.sum(kept, axis=0, keepdims=True), jnp.sum(kept, axis=1, keepdims=True)


def scale_system(a_ref, product):
    rank = product.shape[0]
    eye = lax.broadcasted_iota(jnp.int32, (rank, rank), 0) == lax.broadcasted_iota(jnp.int32, (rank, rank), 1)
    system = product + jnp.where(eye, ridge_term, 0.0)
    along, down = diagonal(system)
    along, down = lax.rsqrt(along), lax.rsqrt(down)
    a_ref[...] = system * down * along
    return along


def kernel(
    n_x, n_z, total_a, total_b,
    t_hbm, b_ref, c_ref,
    hat_a_ref, w_a_ref, hat_b_ref, w_b_ref,
    t_f32, t_hi, t_lo, bz, bfull, bst, call, pb, pbc, hs, pby, gb, gc, ma, ra, pa, pg, gz, gs, ga, sysm, scl, iw,
    mbt, mb, rb1, mb1, rb2, sq, sqp, sqs, sqz,
    t_sem, send_sem, recv_sem,
):
    depth, height, width = t_f32.shape
    rank = c_ref.shape[1]
    ia, ja, ka = lax.axis_index("ia"), lax.axis_index("ja"), lax.axis_index("ka")
    z, yl = lax.div(ia, 2), lax.rem(ia, 2)
    yh, core = lax.div(ja, 2), lax.rem(ja, 2)
    n_s = 4 * n_x
    n_q = 2 * n_s
    n_g = 2 * n_x
    s = ja * n_x + ka
    q = yl * n_s + s
    g = yl * n_x + ka

    def plane_peer(d):
        yl2 = lax.rem(yl + lax.div(d, n_s), 2)
        ja2 = lax.rem(ja + lax.rem(lax.div(d, n_x), 4), 4)
        ka2 = lax.rem(ka + lax.rem(d, n_x), n_x)
        return yl2 * n_s + ja2 * n_x + ka2, (z * 2 + yl2, ja2, ka2)

    def group_peer(d):
        yl2 = lax.rem(yl + lax.div(d, n_x), 2)
        ka2 = lax.rem(ka + lax.rem(d, n_x), n_x)
        return yl2 * n_x + ka2, (z * 2 + yl2, ja, ka2)

    def share_peer(d):
        ja2 = lax.rem(ja + lax.div(d, n_x), 4)
        ka2 = lax.rem(ka + lax.rem(d, n_x), n_x)
        return ja2 * n_x + ka2, (ia, ja2, ka2)

    def z_peer(d):
        z2 = lax.rem(z + d, n_z)
        return z2, (z2 * 2 + yl, ja, ka)

    def x_peer(d):
        ka2 = lax.rem(ka + d, n_x)
        return ka2, (ia, ja, ka2)

    def send(stage, src, dst, device):
        pltpu.make_async_remote_copy(
            src_ref=src, dst_ref=dst, send_sem=send_sem.at[stage], recv_sem=recv_sem.at[stage],
            device_id=device, device_id_type=MESH,
        ).start()

    def fan(stage, count, peer, src, dst):
        def body(d, carry):
            where, device = peer(d)
            send(stage, src(where), dst, device)
            return carry

        lax.fori_loop(1, count, body, 0)

    def arrived(stage, ref):
        pltpu.make_async_copy(ref, ref, recv_sem.at[stage]).wait()

    def sent(stage, ref):
        pltpu.make_async_copy(ref, ref, send_sem.at[stage]).wait()

    n_chunk = t_sem.shape[0]
    per = depth // n_chunk
    loads = [
        pltpu.make_async_copy(t_hbm.at[pl.ds(i * per, per)], t_f32.at[pl.ds(i * per, per)], t_sem.at[i])
        for i in range(n_chunk)
    ]
    for load in loads:
        load.start()

    barrier = pltpu.get_barrier_semaphore()

    def greet(peer):
        def body(d, carry):
            pl.semaphore_signal(barrier, inc=1, device_id=peer(d)[1], device_id_type=MESH)
            return carry

        return body

    lax.fori_loop(1, n_z, greet(z_peer), 0)
    lax.fori_loop(1, n_q, greet(plane_peer), 0)
    pl.semaphore_wait(barrier, n_q + n_z - 2)

    fan(0, n_z, z_peer, lambda _: b_ref, bz.at[z])
    fan(1, n_x, x_peer, lambda _: c_ref, call.at[ka])
    bz[z] = b_ref[...]
    call[ka] = c_ref[...]

    def cut(first, last):
        def body(k, carry):
            hi, lo = split2(t_f32[k])
            t_hi[k] = hi
            t_lo[k] = lo
            return carry

        lax.fori_loop(first, last, body, 0)

    early = n_chunk // 2
    for i in range(early):
        loads[i].wait()
        cut(i * per, (i + 1) * per)
    arrived(0, bz.at[pl.ds(0, n_z - 1)])
    fan(2, n_g, group_peer, lambda _: bz, bfull.at[:, g])
    bfull[:, g] = bz[...]
    for i in range(early, n_chunk):
        loads[i].wait()
        cut(i * per, (i + 1) * per)
    if n_x > 1:
        arrived(1, call.at[pl.ds(0, n_x - 1)])
    call_rows = call[...].reshape(n_x * depth, rank)
    gc[...] = lax.dot_general(call_rows, call_rows, TN, precision=HIGH, preferred_element_type=F32)

    arrived(2, bfull.at[:, pl.ds(0, n_g - 1)])
    rows_b = bfull[...].reshape(width, rank)
    pb[...] = lax.dot_general(rows_b, rows_b, TN, precision=HIGH, preferred_element_type=F32).reshape(pb.shape)
    sibling = (ia, ja + 1 - 2 * core, ka)
    across = (z * 2 + 1 - yl, ja + 2 - 4 * yh, ka)
    send(3, pb.at[1 - core], pbc, sibling)
    hi, lo = split2(rows_b)
    bst[...] = jnp.concatenate([hi, lo, hi], axis=0)
    ma[...] = jnp.zeros_like(ma)

    def first_mode(i, carry):
        k0 = i * per
        th = t_hi[pl.ds(k0, per)].reshape(per * height, width)
        tl = t_lo[pl.ds(k0, per)].reshape(per * height, width)
        along = jnp.dot(jnp.concatenate([th, th, tl], axis=1), bst[...], preferred_element_type=F32)
        total = ma[...].reshape(height, rank)
        for j in range(per):
            total = total + along[j * height : (j + 1) * height] * c_ref[pl.ds(k0 + j, 1), :]
        ma[...] = total.reshape(ma.shape)
        return carry

    lax.fori_loop(0, early, first_mode, 0)
    arrived(3, pbc)
    hs[...] = pb[core] + pbc[...]
    send(4, hs, pby, across)
    lax.fori_loop(early, n_chunk, first_mode, 0)
    fan(5, n_s, share_peer, lambda where: ma.at[where], ra.at[s])
    ra[s] = ma[s]
    arrived(4, pby)
    gb[core] = hs[...] + pby[...]
    send(6, gb.at[core], gb.at[core], sibling)
    arrived(6, gb.at[0])

    scl[...] = scale_system(sysm, gb[...].reshape(rank, rank) * gc[...])
    sweep_panels(sysm, 0, rank // NB)
    arrived(5, ra.at[pl.ds(0, n_s - 1)])
    share_a = jnp.sum(ra[...], axis=0)
    raw_a = -jnp.dot(share_a * scl[...], sysm[...], precision=HIGH, preferred_element_type=F32) * scl[...]

    pa[q] = raw_a
    fan(7, n_q, plane_peer, lambda _: pa.at[q], pa.at[q])
    arrived(7, pa.at[pl.ds(0, n_q - 1)])
    rows_a = pa[...].reshape(n_q * 8, rank)
    pg[...] = lax.dot_general(rows_a, rows_a, TN, precision=HIGH, preferred_element_type=F32).reshape(pg.shape)
    fan(8, n_z, z_peer, lambda _: pg.at[q], gz.at[z])
    gz[z] = pg[q]
    mbt[...] = jnp.zeros_like(mbt)

    def second_mode(i, carry):
        k0 = i * per
        rows = pa[pl.ds(yl * n_s, n_s)].reshape(height, rank)
        both = jnp.concatenate([rows * c_ref[pl.ds(k0 + j, 1), :] for j in range(per)], axis=0)
        hi, lo = split2(both)
        th = t_hi[pl.ds(k0, per)].reshape(per * height, width)
        tl = t_lo[pl.ds(k0, per)].reshape(per * height, width)
        mbt[...] += lax.dot_general(
            jnp.concatenate([hi, lo, hi], axis=0), jnp.concatenate([th, th, tl], axis=0), TN,
            preferred_element_type=F32,
        )
        return carry

    lax.fori_loop(0, early, second_mode, 0)
    arrived(8, gz.at[pl.ds(0, n_z - 1)])
    gs[...] = jnp.sum(gz[...], axis=0)
    fan(9, n_q, plane_peer, lambda _: gs, ga.at[q])
    ga[q] = gs[...]
    lax.fori_loop(early, n_chunk, second_mode, 0)
    mb[...] = mbt[...].T.reshape(mb.shape)
    fan(10, n_g, group_peer, lambda where: mb.at[:, where], rb1.at[g])
    rb1[g] = mb[:, g]

    arrived(9, ga.at[pl.ds(0, n_q - 1)])
    gram = ga[...].reshape(rank, rank)
    along, down = diagonal(gram)
    weight_a = jnp.sqrt(along * (1.0 / total_a) + epsilon)
    iw[...] = 1.0 / weight_a
    w_a_ref[...] = weight_a
    hat_a_ref[...] = pa[q] / weight_a
    down = 1.0 / jnp.sqrt(down * (1.0 / total_a) + epsilon)
    scl[...] = scale_system(sysm, gram * down * iw[...] * gc[...])
    middle = rank // NB // 2
    sweep_panels(sysm, 0, middle)
    arrived(10, rb1.at[pl.ds(0, n_g - 1)])
    mb1[...] = jnp.sum(rb1[...], axis=0)
    fan(11, n_z, z_peer, lambda where: mb1.at[where], rb2.at[z])
    rb2[z] = mb1[z]
    sweep_panels(sysm, middle, rank // NB)
    arrived(11, rb2.at[pl.ds(0, n_z - 1)])
    share_b = jnp.sum(rb2[...], axis=0)
    raw_b = -jnp.dot(share_b * iw[...] * scl[...], sysm[...], precision=HIGH, preferred_element_type=F32) * scl[...]

    sq[...] = jnp.sum(raw_b * raw_b, axis=0, keepdims=True)
    fan(12, n_q, plane_peer, lambda _: sq, sqp.at[q])
    sqp[q] = sq[...]
    arrived(12, sqp.at[pl.ds(0, n_q - 1)])
    sqs[...] = jnp.sum(sqp[...], axis=0)
    fan(13, n_z, z_peer, lambda _: sqs, sqz.at[z])
    sqz[z] = sqs[...]
    arrived(13, sqz.at[pl.ds(0, n_z - 1)])
    weight_b = jnp.sqrt(jnp.sum(sqz[...], axis=0) * (1.0 / total_b) + epsilon)
    w_b_ref[...] = weight_b
    hat_b_ref[...] = raw_b / weight_b

    sent(0, bz.at[pl.ds(0, n_z - 1)])
    if n_x > 1:
        sent(1, call.at[pl.ds(0, n_x - 1)])
    sent(2, bfull.at[:, pl.ds(0, n_g - 1)])
    sent(3, pbc)
    sent(4, pby)
    sent(5, ra.at[pl.ds(0, n_s - 1)])
    sent(6, gb.at[0])
    sent(7, pa.at[pl.ds(0, n_q - 1)])
    sent(8, gz.at[pl.ds(0, n_z - 1)])
    sent(9, ga.at[pl.ds(0, n_q - 1)])
    sent(10, rb1.at[pl.ds(0, n_g - 1)])
    sent(11, rb2.at[pl.ds(0, n_z - 1)])
    sent(12, sqp.at[pl.ds(0, n_q - 1)])
    sent(13, sqz.at[pl.ds(0, n_z - 1)])


def local(tensor, factor_b, factor_c):
    depth, height, width = tensor.shape
    rank = factor_c.shape[1]
    n_x, n_z = lax.axis_size("ka"), lax.axis_size("ia") // 2
    n_s, n_q, n_g = 4 * n_x, 8 * n_x, 2 * n_x
    part = rank // n_q
    n_chunk = 6
    v = pltpu.VMEM
    out = jax.ShapeDtypeStruct
    vmem = pl.BlockSpec(memory_space=pltpu.VMEM)
    hat_a, weight_a, hat_b, weight_b = pl.pallas_call(
        functools.partial(kernel, n_x, n_z, height * lax.axis_size("ia"), width * lax.axis_size("ja")),
        out_shape=[out((8, rank), F32), out((1, rank), F32), out((8, rank), F32), out((1, rank), F32)],
        in_specs=[pl.BlockSpec(memory_space=pl.ANY), vmem, vmem],
        out_specs=[vmem] * 4,
        scratch_shapes=[
            v((depth, height, width), F32),
            v((depth, height, width), BF16),
            v((depth, height, width), BF16),
            v((n_z, 8, rank), F32),
            v((n_z, n_g, 8, rank), F32),
            v((3 * width, rank), BF16),
            v((n_x, depth, rank), F32),
            v((2, rank // 2, rank), F32),
            v((rank // 2, rank), F32),
            v((rank // 2, rank), F32),
            v((rank // 2, rank), F32),
            v((2, rank // 2, rank), F32),
            v((rank, rank), F32),
            v((n_s, 8, rank), F32),
            v((n_s, 8, rank), F32),
            v((n_q, 8, rank), F32),
            v((n_q, part, rank), F32),
            v((n_z, part, rank), F32),
            v((part, rank), F32),
            v((n_q, part, rank), F32),
            v((rank, rank), F32),
            v((1, rank), F32),
            v((1, rank), F32),
            v((rank, width), F32),
            v((n_z, n_g, 8, rank), F32),
            v((n_g, n_z, 8, rank), F32),
            v((n_z, 8, rank), F32),
            v((n_z, 8, rank), F32),
            v((1, rank), F32),
            v((n_q, 1, rank), F32),
            v((1, rank), F32),
            v((n_z, 1, rank), F32),
            pltpu.SemaphoreType.DMA((n_chunk,)),
            pltpu.SemaphoreType.DMA((14,)),
            pltpu.SemaphoreType.DMA((14,)),
        ],
        compiler_params=pltpu.CompilerParams(
            collective_id=0, has_side_effects=True, vmem_limit_bytes=40 * 1024 * 1024
        ),
    )(tensor, factor_b, factor_c)
    return hat_a, weight_a.reshape(rank), hat_b, weight_b.reshape(rank)


def solution(mesh):
    return jax.shard_map(
        local,
        mesh=mesh,
        in_specs=(P("ka", "ia", "ja"), P(("ja", "ia", "ka"), None), P("ka", None)),
        out_specs=(P(("ia", "ja", "ka"), None), P(), P(("ja", "ia", "ka"), None), P()),
        check_vma=False,
    )
```

time: 904 us -> 87.4 us (0.10)
  waiting for transfers between devices: 397 us -> 0 us
  blocking collectives: 331 us -> 0 us
  other arithmetic: 111 us -> 0 us
  Pallas kernels: 0 us -> 80 us
  matrix products: 32.4 us -> 0 us
  between operations: 18.3 us -> 0.65 us
    psum x3 -> x0, waiting for transfers between devices: 397 us -> none  [the longest x1 238 us: local(): lax.psum(jnp.dot(hat_a.T, hat_a, precision=high, preferred_element_type=j...]
    psum x2 -> x0, blocking collectives: 167 us -> none  [the longest x1 89.4 us: local(): squares_b = lax.psum(jnp.sum(raw_b * raw_b, axis=0), ('ia', 'ja', 'ka'))]
    all_gather x2 -> x0, blocking collectives: 164 us -> none  [the longest x1 135 us: local(): lax.all_gather(factor_b, ('ia', 'ka'), axis=0, tiled=True)]
    another operation x18 -> x0, other arithmetic: 108 us -> none  [the longest x13 68.6 us: solve_rows(): lower = jnp.linalg.cholesky(system)]
    pallas_call x0 -> x1, Pallas kernels: none -> 80 us  [local(): pl.pallas_call(functools.partial(kernel, n_x, n_z, height * lax.axis_size...]
    dot_general x5 -> x0, matrix products: 26.5 us -> none  [the longest x1 13 us: local(): jnp.einsum('kij,ir->kjr', tensor, lax.all_gather(hat_a, ('ja', 'ka'), axi...]
  transfers between devices with their start and end apart: 5 -> 0, of which waited for: 3 -> 0; matrix products, arithmetic and copies ran while one was open for 16% -> 0% of each run, Pallas kernels for 0% -> 0%
where the time goes in v1:
time: 87.4 us; the launch traced here: 87.2 us
  Pallas kernels  80 us (92%)
  local copies, waits for them, and re-layouts  6.54 us (7%)
    pallas_call x1, Pallas kernels, local(): pl.pallas_call(functools.partial(kernel, n_x, n_z, height * lax.axis_size...  80 us
    unnamed x10, local copies, waits for them, and re-layouts  6.54 us

profile of v1, /device:TPU:1, one launch (start us, length us, event | category | flops | bytes accessed | tf_op | source)
XLA Modules:
  0.0 87.2 jit_solution(8627151750815201561)
XLA Ops:
  0.6 0.0 copy-start
  0.6 2.8 %copy-done = f32[24,128,512]{2,1,0:T(8,128)S(1)} copy-done((f32[24,128,512]{2,1,0:T(8,128)S(1)}, f32[24,128,512]{2,1,0:T(8,128)}, u32[]{:S(2)}) %copy-start) | copy-done | bytes 6291480
  3.4 0.0 copy-start.1
  3.4 0.7 copy-done.1
  4.2 0.0 copy-start.2
  4.2 0.7 copy-done.2
  4.9 80.0 %shard_map.66 = (f32[8,256]{1,0:T(8,128)S(1)}, f32[1,256]{1,0:T(1,128)S(1)}, f32[8,256]{1,0:T(8,128)S(1)}, f32[1,256]{1,0:T(1,128)S(1)}) custom-call(f32[24,128,512]{2,1,0:T(8,128)S(1)} %copy-done, f32[8,256]{1,0:T(8,128)S(1)} %copy-done.2, f32[24,256]{1,0:T(8,128)S(1)} %copy-done.1), custom_call_target="tpu_custom_call" | custom-call | tf_op jit(solution)/shard_map/pallas_call | solution.py:343
  84.9 0.6 copy.11
  85.5 0.6 copy.12
  86.0 0.6 copy.13
  86.6 0.6 copy.14
Async XLA Ops:
  0.6 2.8 %copy-start = (f32[24,128,512]{2,1,0:T(8,128)S(1)}, f32[24,128,512]{2,1,0:T(8,128)}, u32[]{:S(2)}) copy-start(f32[24,128,512]{2,1,0:T(8,128)} %t_hbm.1) | copy-start | bytes 18874372
  3.4 0.7 copy-start.1
  4.2 0.7 copy-start.2

commit v2 on v1

--- a/solution.py
+++ b/solution.py
@@ -14,7 +14,8 @@
 HIGH = lax.Precision.HIGHEST
 F32 = jnp.float32
 BF16 = jnp.bfloat16
-NB = 16
+VMEM_LIMIT = 65000000
+NB = 32
 TN = (((0,), (0,)), ((), ()))
 
 
@@ -30,15 +31,46 @@
     return hi, mid, (rest - mid.astype(F32)).astype(BF16)
 
 
+def every(v):
+    return jnp.broadcast_to(v, (8, 128))
+
+
+def inverse8(e):
+    get = lambda i, j: e[min(i, j)][max(i, j)]
+    for p in range(0, 8, 2):
+        a, b, c = e[p][p], e[p][p + 1], e[p + 1][p + 1]
+        det = a * c - b * b
+        inv = pl.reciprocal(det, approx=True)
+        inv = inv * (2.0 - det * inv)
+        inv = inv * (2.0 - det * inv)
+        fa, fb, fc = a * inv, b * inv, c * inv
+        others = [i for i in range(8) if i not in (p, p + 1)]
+        old = {i: (get(i, p), get(i, p + 1)) for i in others}
+        new = {i: (fc * old[i][0] - fb * old[i][1], fa * old[i][1] - fb * old[i][0]) for i in others}
+        for i in others:
+            for j in others:
+                if i <= j:
+                    e[i][j] = e[i][j] - new[i][0] * old[j][0] - new[i][1] * old[j][1]
+        for i in others:
+            e[min(i, p)][max(i, p)], e[min(i, p + 1)][max(i, p + 1)] = new[i]
+        e[p][p], e[p][p + 1], e[p + 1][p + 1] = -fc, fb, -fa
+    return e
+
+
+def sum_of(terms):
+    while len(terms) > 1:
+        terms = [sum(terms[i : i + 2][1:], terms[i]) for i in range(0, len(terms), 2)]
+    return terms[0]
+
+
 def sweep_panels(a_ref, first, last):
     rank = a_ref.shape[0]
+    parts = rank // 128
     lane = lax.broadcasted_iota(jnp.int32, (NB, rank), 1)
     row = lax.broadcasted_iota(jnp.int32, (NB, rank), 0)
-    row1 = lax.broadcasted_iota(jnp.int32, (NB, 128), 0)
+    row8 = lax.broadcasted_iota(jnp.int32, (8, 128), 0)
     lane_all = lax.broadcasted_iota(jnp.int32, (rank, rank), 1)
-
-    def wide(v):
-        return jnp.concatenate([v] * (rank // 128), axis=1)
+    groups = NB // 8
 
     def panel(b, carry):
         r0 = pl.multiple_of(b * NB, NB)
@@ -46,26 +78,30 @@
         base = pl.multiple_of(lax.div(r0, 128) * 128, 128)
         half = a_ref[pl.ds(r0, NB), pl.ds(base, 128)]
         d = pltpu.roll(half, lax.rem(128 - (r0 - base), 128), 1)
-        cols = [jnp.broadcast_to(d[:, j : j + 1], (NB, 128)) for j in range(NB)]
         inside = (lane >= r0) & (lane < r0 + NB)
         rz = jnp.where(inside, 0.0, r)
-        q = jnp.where(inside, jnp.where(lane - r0 == row, -1.0, 0.0), r)
-        for p in range(0, NB, 2):
-            cp, cq = cols[p], cols[p + 1]
-            a, b1, e = cp[p : p + 1], cp[p + 1 : p + 2], cq[p + 1 : p + 2]
-            inv = 1.0 / (a * e - b1 * b1)
-            fa, fb, fe = a * inv, b1 * inv, e * inv
-
-            def apply(y, ma, mb, me, mp, mq, rows):
-                yp, yq = y[p : p + 1], y[p + 1 : p + 2]
-                np_ = me * yp - mb * yq
-                nq_ = ma * yq - mb * yp
-                new = y - mp * np_ - mq * nq_
-                return jnp.where(rows == p, np_, jnp.where(rows == p + 1, nq_, new))
-
-            for j in range(p + 2, NB):
-                cols[j] = apply(cols[j], fa, fb, fe, cp, cq, row1)
-            q = apply(q, wide(fa), wide(fb), wide(fe), wide(cp), wide(cq), row)
+        start = jnp.where(inside, jnp.where(lane - r0 == row, -1.0, 0.0), r)
+        x = [
+            [d[8 * m : 8 * m + 8]] + [start[8 * m : 8 * m + 8, 128 * h : 128 * h + 128] for h in range(parts)]
+            for m in range(groups)
+        ]
+        for i in range(groups):
+            cols = [every(x[i][0][:, 8 * i + j : 8 * i + j + 1]) for j in range(8)]
+            e = [[every(cols[j][k : k + 1]) if k <= j else None for j in range(8)] for k in range(8)]
+            e = inverse8(e)
+            weights = []
+            for j in range(8):
+                w = e[0][j]
+                for k in range(1, 8):
+                    w = jnp.where(row8 == k, e[min(k, j)][max(k, j)], w)
+                weights.append(w)
+            x[i] = [-sum_of([weights[j] * every(y[j : j + 1]) for j in range(8)]) for y in x[i]]
+            spread = [[every(y[j : j + 1]) for j in range(8)] for y in x[i]]
+            for m in range(groups):
+                if m != i:
+                    left = [every(x[m][0][:, 8 * i + j : 8 * i + j + 1]) for j in range(8)]
+                    x[m] = [y - sum_of([left[j] * s[j] for j in range(8)]) for y, s in zip(x[m], spread)]
+        q = jnp.concatenate([jnp.concatenate(x[m][1:], axis=1) for m in range(groups)], axis=0)
         r1, r2, r3 = split3(rz)
         q1, q2, q3 = split3(q)
         left = jnp.concatenate([r1, r1, r2, r2, r1, r3], axis=0)
@@ -97,11 +133,11 @@
 
 def kernel(
     n_x, n_z, total_a, total_b,
-    t_hbm, b_ref, c_ref,
-    hat_a_ref, w_a_ref, hat_b_ref, w_b_ref,
-    t_f32, t_hi, t_lo, bz, bfull, bst, call, pb, pbc, hs, pby, gb, gc, ma, ra, pa, pg, gz, gs, ga, sysm, scl, iw,
+    t_hbm, b_hbm, c_hbm,
+    hat_a_hbm, w_a_hbm, hat_b_hbm, w_b_hbm,
+    hat_a_ref, w_a_ref, hat_b_ref, w_b_ref, b_ref, c_ref, t_f32, t_hi, t_lo, bz, bfull, bst, call, pb, pbc, hs, pby, gb, gc, ma, ra, pa, pg, gz, gs, ga, sysm, scl, iw,
     mbt, mb, rb1, mb1, rb2, sq, sqp, sqs, sqz,
-    t_sem, send_sem, recv_sem,
+    t_sem, out_sem, send_sem, recv_sem,
 ):
     depth, height, width = t_f32.shape
     rank = c_ref.shape[1]
@@ -159,13 +195,14 @@
     def sent(stage, ref):
         pltpu.make_async_copy(ref, ref, send_sem.at[stage]).wait()
 
-    n_chunk = t_sem.shape[0]
+    n_chunk = t_sem.shape[0] - 2
     per = depth // n_chunk
     loads = [
         pltpu.make_async_copy(t_hbm.at[pl.ds(i * per, per)], t_f32.at[pl.ds(i * per, per)], t_sem.at[i])
         for i in range(n_chunk)
     ]
-    for load in loads:
+    small = [pltpu.make_async_copy(b_hbm, b_ref, t_sem.at[n_chunk]), pltpu.make_async_copy(c_hbm, c_ref, t_sem.at[n_chunk + 1])]
+    for load in small + loads:
         load.start()
 
     barrier = pltpu.get_barrier_semaphore()
@@ -181,6 +218,8 @@
     lax.fori_loop(1, n_q, greet(plane_peer), 0)
     pl.semaphore_wait(barrier, n_q + n_z - 2)
 
+    for load in small:
+        load.wait()
     fan(0, n_z, z_peer, lambda _: b_ref, bz.at[z])
     fan(1, n_x, x_peer, lambda _: c_ref, call.at[ka])
     bz[z] = b_ref[...]
@@ -288,6 +327,14 @@
     iw[...] = 1.0 / weight_a
     w_a_ref[...] = weight_a
     hat_a_ref[...] = pa[q] / weight_a
+    results = [
+        pltpu.make_async_copy(have, want, out_sem.at[i])
+        for i, (have, want) in enumerate(
+            [(hat_a_ref, hat_a_hbm), (w_a_ref, w_a_hbm), (hat_b_ref, hat_b_hbm), (w_b_ref, w_b_hbm)]
+        )
+    ]
+    for result in results[:2]:
+        result.start()
     down = 1.0 / jnp.sqrt(down * (1.0 / total_a) + epsilon)
     scl[...] = scale_system(sysm, gram * down * iw[...] * gc[...])
     middle = rank // NB // 2
@@ -312,6 +359,8 @@
     weight_b = jnp.sqrt(jnp.sum(sqz[...], axis=0) * (1.0 / total_b) + epsilon)
     w_b_ref[...] = weight_b
     hat_b_ref[...] = raw_b / weight_b
+    for result in results[2:]:
+        result.start()
 
     sent(0, bz.at[pl.ds(0, n_z - 1)])
     if n_x > 1:
@@ -328,6 +377,16 @@
     sent(11, rb2.at[pl.ds(0, n_z - 1)])
     sent(12, sqp.at[pl.ds(0, n_q - 1)])
     sent(13, sqz.at[pl.ds(0, n_z - 1)])
+    for result in results:
+        result.wait()
+
+
+def finish(*refs):
+    copies = [pltpu.make_async_copy(refs[i], refs[4 + i], refs[8].at[i]) for i in range(4)]
+    for copy in copies:
+        copy.start()
+    for copy in copies:
+        copy.wait()
 
 
 def local(tensor, factor_b, factor_c):
@@ -339,13 +398,20 @@
     n_chunk = 6
     v = pltpu.VMEM
     out = jax.ShapeDtypeStruct
-    vmem = pl.BlockSpec(memory_space=pltpu.VMEM)
-    hat_a, weight_a, hat_b, weight_b = pl.pallas_call(
+    hbm = pl.BlockSpec(memory_space=pltpu.HBM)
+    results = [out((8, rank), F32), out((1, rank), F32), out((8, rank), F32), out((1, rank), F32)]
+    found = pl.pallas_call(
         functools.partial(kernel, n_x, n_z, height * lax.axis_size("ia"), width * lax.axis_size("ja")),
-        out_shape=[out((8, rank), F32), out((1, rank), F32), out((8, rank), F32), out((1, rank), F32)],
-        in_specs=[pl.BlockSpec(memory_space=pl.ANY), vmem, vmem],
-        out_specs=[vmem] * 4,
+        out_shape=results,
+        in_specs=[hbm] * 3,
+        out_specs=[hbm] * 4,
         scratch_shapes=[
+            v((8, rank), F32),
+            v((1, rank), F32),
+            v((8, rank), F32),
+            v((1, rank), F32),
+            v((8, rank), F32),
+            v((depth, rank), F32),
             v((depth, height, width), F32),
             v((depth, height, width), BF16),
             v((depth, height, width), BF16),
@@ -378,14 +444,23 @@
             v((n_q, 1, rank), F32),
             v((1, rank), F32),
             v((n_z, 1, rank), F32),
-            pltpu.SemaphoreType.DMA((n_chunk,)),
+            pltpu.SemaphoreType.DMA((n_chunk + 2,)),
+            pltpu.SemaphoreType.DMA((4,)),
             pltpu.SemaphoreType.DMA((14,)),
             pltpu.SemaphoreType.DMA((14,)),
         ],
         compiler_params=pltpu.CompilerParams(
-            collective_id=0, has_side_effects=True, vmem_limit_bytes=40 * 1024 * 1024
+            collective_id=0, has_side_effects=True, vmem_limit_bytes=VMEM_LIMIT
         ),
     )(tensor, factor_b, factor_c)
+    hat_a, weight_a, hat_b, weight_b = pl.pallas_call(
+        finish,
+        out_shape=results,
+        in_specs=[hbm] * 4,
+        out_specs=[hbm] * 4,
+        scratch_shapes=[pltpu.SemaphoreType.DMA((4,))],
+        compiler_params=pltpu.CompilerParams(vmem_limit_bytes=VMEM_LIMIT),
+    )(*found)
     return hat_a, weight_a.reshape(rank), hat_b, weight_b.reshape(rank)
 
 

time: 87.4 us -> 89 us (1.018)
  Pallas kernels: 80 us -> 88.3 us
  local copies, waits for them, and re-layouts: 6.54 us -> 0 us
    pallas_call x1, Pallas kernels: 80 us -> 86.6 us  [local(): pl.pallas_call(functools.partial(kernel, n_x, n_z, height * lax.axis_size...]
    unnamed x10 -> x0, local copies, waits for them, and re-layouts: 6.54 us -> none
    pallas_call x0 -> x1, Pallas kernels: none -> 1.7 us  [local(): pl.pallas_call(finish, out_shape=results, in_specs=[hbm] * 4, out_specs=[...]
where the time goes in v2:
time: 89 us; the launch traced here: 88.9 us
  Pallas kernels  88.3 us (99%)
    pallas_call x1, Pallas kernels, local(): pl.pallas_call(functools.partial(kernel, n_x, n_z, height * lax.axis_size...  86.6 us

profile of v2, /device:TPU:1, one launch (start us, length us, event | category | flops | bytes accessed | tf_op | source)
XLA Modules:
  0.0 88.9 jit_solution(18168194368153171155)
XLA Ops:
  0.6 86.6 %shard_map.66 = (f32[8,256]{1,0:T(8,128)}, f32[1,256]{1,0:T(1,128)}, f32[8,256]{1,0:T(8,128)}, f32[1,256]{1,0:T(1,128)}) custom-call(f32[24,128,512]{2,1,0:T(8,128)} %t_hbm.1, f32[8,256]{1,0:T(8,128)} %b_hbm.1, f32[24,256]{1,0:T(8,128)} %c_hbm.1), custom_call_target="tpu_custom_call" | custom-call | tf_op jit(solution)/shard_map/pallas_call | solution.py:403
  87.2 1.7 %shard_map.67 = (f32[8,256]{1,0:T(8,128)}, f32[1,256]{1,0:T(1,128)}, f32[8,256]{1,0:T(8,128)}, f32[1,256]{1,0:T(1,128)}) custom-call(f32[8,256]{1,0:T(8,128)} %get-tuple-element.12.refs_0_, f32[1,256]{1,0:T(1,128)} %get-tuple-element.13.refs_1_, f32[8,256]{1,0:T(8,128)} %get-tuple-element.14.refs_2_, f32[1,256]{1,0:T(1,128)} %get-tuple-element.15.refs_3_), custom_call_target="tpu_custom_call" | custom-call | tf_op jit(solution)/shard_map/pallas_call | solution.py:456

commit v3 on v2

--- a/solution.py
+++ b/solution.py
@@ -35,49 +35,27 @@
     return jnp.broadcast_to(v, (8, 128))
 
 
-def inverse8(e):
-    get = lambda i, j: e[min(i, j)][max(i, j)]
-    for p in range(0, 8, 2):
-        a, b, c = e[p][p], e[p][p + 1], e[p + 1][p + 1]
-        det = a * c - b * b
-        inv = pl.reciprocal(det, approx=True)
-        inv = inv * (2.0 - det * inv)
-        inv = inv * (2.0 - det * inv)
-        fa, fb, fc = a * inv, b * inv, c * inv
-        others = [i for i in range(8) if i not in (p, p + 1)]
-        old = {i: (get(i, p), get(i, p + 1)) for i in others}
-        new = {i: (fc * old[i][0] - fb * old[i][1], fa * old[i][1] - fb * old[i][0]) for i in others}
-        for i in others:
-            for j in others:
-                if i <= j:
-                    e[i][j] = e[i][j] - new[i][0] * old[j][0] - new[i][1] * old[j][1]
-        for i in others:
-            e[min(i, p)][max(i, p)], e[min(i, p + 1)][max(i, p + 1)] = new[i]
-        e[p][p], e[p][p + 1], e[p + 1][p + 1] = -fc, fb, -fa
-    return e
-
-
-def sum_of(terms):
-    while len(terms) > 1:
-        terms = [sum(terms[i : i + 2][1:], terms[i]) for i in range(0, len(terms), 2)]
-    return terms[0]
-
-
-def sweep_panels(a_ref, first, last):
+def sweep_panels(a_ref, lt_ref, rt_ref, q_ref, first, last):
     rank = a_ref.shape[0]
     parts = rank // 128
+    groups = NB // 8
     lane = lax.broadcasted_iota(jnp.int32, (NB, rank), 1)
     row = lax.broadcasted_iota(jnp.int32, (NB, rank), 0)
     row8 = lax.broadcasted_iota(jnp.int32, (8, 128), 0)
-    lane_all = lax.broadcasted_iota(jnp.int32, (rank, rank), 1)
-    groups = NB // 8
 
     def panel(b, carry):
         r0 = pl.multiple_of(b * NB, NB)
-        r = a_ref[pl.ds(r0, NB), :]
-        base = pl.multiple_of(lax.div(r0, 128) * 128, 128)
-        half = a_ref[pl.ds(r0, NB), pl.ds(base, 128)]
-        d = pltpu.roll(half, lax.rem(128 - (r0 - base), 128), 1)
+        before = (lane >= r0 - NB) & (lane < r0)
+        r = jnp.where(before, 0.0, a_ref[pl.ds(r0, NB), :]) - jnp.dot(
+            lt_ref[pl.ds(r0, NB), :], rt_ref[...], preferred_element_type=F32
+        )
+        base = lax.div(r0, 128)
+        half = r[:, :128]
+        for h in range(1, parts):
+            half = jnp.where(base == h, r[:, 128 * h : 128 * h + 128], half)
+        d = pltpu.roll(half, lax.rem(128 - (r0 - base * 128), 128), 1)
+        catch_up(a_ref, lt_ref, rt_ref, q_ref, b)
+
         inside = (lane >= r0) & (lane < r0 + NB)
         rz = jnp.where(inside, 0.0, r)
         start = jnp.where(inside, jnp.where(lane - r0 == row, -1.0, 0.0), r)
@@ -85,33 +63,51 @@
             [d[8 * m : 8 * m + 8]] + [start[8 * m : 8 * m + 8, 128 * h : 128 * h + 128] for h in range(parts)]
             for m in range(groups)
         ]
-        for i in range(groups):
-            cols = [every(x[i][0][:, 8 * i + j : 8 * i + j + 1]) for j in range(8)]
-            e = [[every(cols[j][k : k + 1]) if k <= j else None for j in range(8)] for k in range(8)]
-            e = inverse8(e)
-            weights = []
-            for j in range(8):
-                w = e[0][j]
-                for k in range(1, 8):
-                    w = jnp.where(row8 == k, e[min(k, j)][max(k, j)], w)
-                weights.append(w)
-            x[i] = [-sum_of([weights[j] * every(y[j : j + 1]) for j in range(8)]) for y in x[i]]
-            spread = [[every(y[j : j + 1]) for j in range(8)] for y in x[i]]
-            for m in range(groups):
-                if m != i:
-                    left = [every(x[m][0][:, 8 * i + j : 8 * i + j + 1]) for j in range(8)]
-                    x[m] = [y - sum_of([left[j] * s[j] for j in range(8)]) for y, s in zip(x[m], spread)]
+        for p in range(0, NB, 2):
+            i, s = p // 8, p % 8
+            left = [every(x[m][0][:, p : p + 1]) for m in range(groups)]
+            right = [every(x[m][0][:, p + 1 : p + 2]) for m in range(groups)]
+            a, c, e = every(left[i][s : s + 1]), every(right[i][s : s + 1]), every(right[i][s + 1 : s + 2])
+            det = a * e - c * c
+            inv = pl.reciprocal(det, approx=True)
+            inv = inv * (2.0 - det * inv)
+            inv = inv * (2.0 - det * inv)
+            fa, fc, fe = a * inv, c * inv, e * inv
+            for v in range(parts + 1):
+                yp, yq = every(x[i][v][s : s + 1]), every(x[i][v][s + 1 : s + 2])
+                wp = fe * yp - fc * yq
+                wq = fa * yq - fc * yp
+                for m in range(groups):
+                    x[m][v] = x[m][v] - left[m] * wp - right[m] * wq
+                x[i][v] = jnp.where(row8 == s, wp, jnp.where(row8 == s + 1, wq, x[i][v]))
         q = jnp.concatenate([jnp.concatenate(x[m][1:], axis=1) for m in range(groups)], axis=0)
         r1, r2, r3 = split3(rz)
         q1, q2, q3 = split3(q)
-        left = jnp.concatenate([r1, r1, r2, r2, r1, r3], axis=0)
-        right = jnp.concatenate([q1, q2, q1, q2, q3, q1], axis=0)
-        update = lax.dot_general(left, right, TN, preferred_element_type=F32)
-        a_ref[...] = jnp.where((lane_all >= r0) & (lane_all < r0 + NB), 0.0, a_ref[...]) - update
-        a_ref[pl.ds(r0, NB), :] = q
+        lt_ref[...] = jnp.concatenate([r1, r1, r2, r2, r1, r3], axis=0).T
+        rt_ref[...] = jnp.concatenate([q1, q2, q1, q2, q3, q1], axis=0)
+        q_ref[...] = q
         return carry
 
     lax.fori_loop(first, last, panel, 0)
+
+
+def catch_up(a_ref, lt_ref, rt_ref, q_ref, b):
+    rank = a_ref.shape[0]
+    r0 = b * NB
+    lane = lax.broadcasted_iota(jnp.int32, (rank, rank), 1)
+    update = jnp.dot(lt_ref[...], rt_ref[...], preferred_element_type=F32)
+    a_ref[...] = jnp.where((lane >= r0 - NB) & (lane < r0), 0.0, a_ref[...]) - update
+    a_ref[pl.ds(pl.multiple_of(jnp.maximum(r0 - NB, 0), NB), NB), :] = q_ref[...]
+
+
+def sweep_begin(a_ref, lt_ref, rt_ref, q_ref):
+    lt_ref[...] = jnp.zeros_like(lt_ref)
+    rt_ref[...] = jnp.zeros_like(rt_ref)
+    q_ref[...] = a_ref[:NB, :]
+
+
+def sweep_end(a_ref, lt_ref, rt_ref, q_ref):
+    catch_up(a_ref, lt_ref, rt_ref, q_ref, a_ref.shape[0] // NB)
 
 
 def diagonal(matrix):
@@ -135,7 +131,7 @@
     n_x, n_z, total_a, total_b,
     t_hbm, b_hbm, c_hbm,
     hat_a_hbm, w_a_hbm, hat_b_hbm, w_b_hbm,
-    hat_a_ref, w_a_ref, hat_b_ref, w_b_ref, b_ref, c_ref, t_f32, t_hi, t_lo, bz, bfull, bst, call, pb, pbc, hs, pby, gb, gc, ma, ra, pa, pg, gz, gs, ga, sysm, scl, iw,
+    hat_a_ref, w_a_ref, hat_b_ref, w_b_ref, b_ref, c_ref, t_f32, t_hi, t_lo, bz, bfull, bst, call, pb, pbc, hs, pby, gb, gc, ma, ra, pa, pg, gz, gs, ga, sysm, lt, rt, qp, scl, iw,
     mbt, mb, rb1, mb1, rb2, sq, sqp, sqs, sqz,
     t_sem, out_sem, send_sem, recv_sem,
 ):
@@ -151,29 +147,29 @@
     q = yl * n_s + s
     g = yl * n_x + ka
 
+    yls = [lax.rem(yl + d, 2) for d in range(2)]
+    jas = [lax.rem(ja + d, 4) for d in range(4)]
+    kas = [lax.rem(ka + d, n_x) for d in range(n_x)]
+    zs = [lax.rem(z + d, n_z) for d in range(n_z)]
+    ias = [z * 2 + yl2 for yl2 in yls]
+
     def plane_peer(d):
-        yl2 = lax.rem(yl + lax.div(d, n_s), 2)
-        ja2 = lax.rem(ja + lax.rem(lax.div(d, n_x), 4), 4)
-        ka2 = lax.rem(ka + lax.rem(d, n_x), n_x)
-        return yl2 * n_s + ja2 * n_x + ka2, (z * 2 + yl2, ja2, ka2)
+        y, j, k = d // n_s, d // n_x % 4, d % n_x
+        return yls[y] * n_s + jas[j] * n_x + kas[k], (ias[y], jas[j], kas[k])
 
     def group_peer(d):
-        yl2 = lax.rem(yl + lax.div(d, n_x), 2)
-        ka2 = lax.rem(ka + lax.rem(d, n_x), n_x)
-        return yl2 * n_x + ka2, (z * 2 + yl2, ja, ka2)
+        y, k = d // n_x, d % n_x
+        return yls[y] * n_x + kas[k], (ias[y], ja, kas[k])
 
     def share_peer(d):
-        ja2 = lax.rem(ja + lax.div(d, n_x), 4)
-        ka2 = lax.rem(ka + lax.rem(d, n_x), n_x)
-        return ja2 * n_x + ka2, (ia, ja2, ka2)
+        j, k = d // n_x, d % n_x
+        return jas[j] * n_x + kas[k], (ia, jas[j], kas[k])
 
     def z_peer(d):
-        z2 = lax.rem(z + d, n_z)
-        return z2, (z2 * 2 + yl, ja, ka)
+        return zs[d], (zs[d] * 2 + yl, ja, ka)
 
     def x_peer(d):
-        ka2 = lax.rem(ka + d, n_x)
-        return ka2, (ia, ja, ka2)
+        return kas[d], (ia, ja, kas[d])
 
     def send(stage, src, dst, device):
         pltpu.make_async_remote_copy(
@@ -182,12 +178,9 @@
         ).start()
 
     def fan(stage, count, peer, src, dst):
-        def body(d, carry):
+        for d in range(1, count):
             where, device = peer(d)
             send(stage, src(where), dst, device)
-            return carry
-
-        lax.fori_loop(1, count, body, 0)
 
     def arrived(stage, ref):
         pltpu.make_async_copy(ref, ref, recv_sem.at[stage]).wait()
@@ -207,15 +200,9 @@
 
     barrier = pltpu.get_barrier_semaphore()
 
-    def greet(peer):
-        def body(d, carry):
+    for count, peer in ((n_z, z_peer), (n_q, plane_peer)):
+        for d in range(1, count):
             pl.semaphore_signal(barrier, inc=1, device_id=peer(d)[1], device_id_type=MESH)
-            return carry
-
-        return body
-
-    lax.fori_loop(1, n_z, greet(z_peer), 0)
-    lax.fori_loop(1, n_q, greet(plane_peer), 0)
     pl.semaphore_wait(barrier, n_q + n_z - 2)
 
     for load in small:
@@ -235,13 +222,10 @@
         lax.fori_loop(first, last, body, 0)
 
     early = n_chunk // 2
-    for i in range(early):
-        loads[i].wait()
-        cut(i * per, (i + 1) * per)
     arrived(0, bz.at[pl.ds(0, n_z - 1)])
     fan(2, n_g, group_peer, lambda _: bz, bfull.at[:, g])
     bfull[:, g] = bz[...]
-    for i in range(early, n_chunk):
+    for i in range(n_chunk):
         loads[i].wait()
         cut(i * per, (i + 1) * per)
     if n_x > 1:
@@ -283,7 +267,10 @@
     arrived(6, gb.at[0])
 
     scl[...] = scale_system(sysm, gb[...].reshape(rank, rank) * gc[...])
-    sweep_panels(sysm, 0, rank // NB)
+    sweep = (sysm, lt, rt, qp)
+    sweep_begin(*sweep)
+    sweep_panels(*sweep, 0, rank // NB)
+    sweep_end(*sweep)
     arrived(5, ra.at[pl.ds(0, n_s - 1)])
     share_a = jnp.sum(ra[...], axis=0)
     raw_a = -jnp.dot(share_a * scl[...], sysm[...], precision=HIGH, preferred_element_type=F32) * scl[...]
@@ -338,12 +325,14 @@
     down = 1.0 / jnp.sqrt(down * (1.0 / total_a) + epsilon)
     scl[...] = scale_system(sysm, gram * down * iw[...] * gc[...])
     middle = rank // NB // 2
-    sweep_panels(sysm, 0, middle)
+    sweep_begin(*sweep)
+    sweep_panels(*sweep, 0, middle)
     arrived(10, rb1.at[pl.ds(0, n_g - 1)])
     mb1[...] = jnp.sum(rb1[...], axis=0)
     fan(11, n_z, z_peer, lambda where: mb1.at[where], rb2.at[z])
     rb2[z] = mb1[z]
-    sweep_panels(sysm, middle, rank // NB)
+    sweep_panels(*sweep, middle, rank // NB)
+    sweep_end(*sweep)
     arrived(11, rb2.at[pl.ds(0, n_z - 1)])
     share_b = jnp.sum(rb2[...], axis=0)
     raw_b = -jnp.dot(share_b * iw[...] * scl[...], sysm[...], precision=HIGH, preferred_element_type=F32) * scl[...]
@@ -433,6 +422,9 @@
             v((part, rank), F32),
             v((n_q, part, rank), F32),
             v((rank, rank), F32),
+            v((rank, 6 * NB), BF16),
+            v((6 * NB, rank), BF16),
+            v((NB, rank), F32),
             v((1, rank), F32),
             v((1, rank), F32),
             v((rank, width), F32),

time: 89 us -> 106 us (1.19)
  Pallas kernels: 88.3 us -> 106 us
    pallas_call x1, Pallas kernels: 86.6 us -> 104 us  [local(): pl.pallas_call(functools.partial(kernel, n_x, n_z, height * lax.axis_size...]
where the time goes in v3:
time: 106 us
  Pallas kernels  106 us (100%)
    pallas_call x1, Pallas kernels, local(): pl.pallas_call(functools.partial(kernel, n_x, n_z, height * lax.axis_size...  104 us

profile of v3, /device:TPU:1, one launch (start us, length us, event | category | flops | bytes accessed | tf_op | source)
XLA Modules:
  0.0 106.3 jit_solution(2937383920417095165)
XLA Ops:
  0.6 104.0 %shard_map.66 = (f32[8,256]{1,0:T(8,128)}, f32[1,256]{1,0:T(1,128)}, f32[8,256]{1,0:T(8,128)}, f32[1,256]{1,0:T(1,128)}) custom-call(f32[24,128,512]{2,1,0:T(8,128)} %t_hbm.1, f32[8,256]{1,0:T(8,128)} %b_hbm.1, f32[24,256]{1,0:T(8,128)} %c_hbm.1), custom_call_target="tpu_custom_call" | custom-call | tf_op jit(solution)/shard_map/pallas_call | solution.py:392
  104.6 1.7 %shard_map.67 = (f32[8,256]{1,0:T(8,128)}, f32[1,256]{1,0:T(1,128)}, f32[8,256]{1,0:T(8,128)}, f32[1,256]{1,0:T(1,128)}) custom-call(f32[8,256]{1,0:T(8,128)} %get-tuple-element.12.refs_0_, f32[1,256]{1,0:T(1,128)} %get-tuple-element.13.refs_1_, f32[8,256]{1,0:T(8,128)} %get-tuple-element.14.refs_2_, f32[1,256]{1,0:T(1,128)} %get-tuple-element.15.refs_3_), custom_call_target="tpu_custom_call" | custom-call | tf_op jit(solution)/shard_map/pallas_call | solution.py:448

commit v4 on v3

--- a/solution.py
+++ b/solution.py
@@ -16,6 +16,7 @@
 BF16 = jnp.bfloat16
 VMEM_LIMIT = 65000000
 NB = 32
+SUB = 16
 TN = (((0,), (0,)), ((), ()))
 
 
@@ -31,83 +32,113 @@
     return hi, mid, (rest - mid.astype(F32)).astype(BF16)
 
 
-def every(v):
-    return jnp.broadcast_to(v, (8, 128))
-
-
-def sweep_panels(a_ref, lt_ref, rt_ref, q_ref, first, last):
+def sweep_half(a_ref, lt_ref, rt_ref, q_ref, tmp_ref, h):
     rank = a_ref.shape[0]
     parts = rank // 128
+    row8 = lax.broadcasted_iota(jnp.int32, (8, 128), 0)
+    lane8 = lax.broadcasted_iota(jnp.int32, (8, 128), 1)
+    lane = lax.broadcasted_iota(jnp.int32, (NB, rank), 1)
     groups = NB // 8
-    lane = lax.broadcasted_iota(jnp.int32, (NB, rank), 1)
-    row = lax.broadcasted_iota(jnp.int32, (NB, rank), 0)
-    row8 = lax.broadcasted_iota(jnp.int32, (8, 128), 0)
-
-    def panel(b, carry):
-        r0 = pl.multiple_of(b * NB, NB)
+    wide = SUB // 8
+    for t in range(128 // NB):
+        l0 = t * NB
+        r0 = pl.multiple_of(h * 128 + l0, NB)
         before = (lane >= r0 - NB) & (lane < r0)
         r = jnp.where(before, 0.0, a_ref[pl.ds(r0, NB), :]) - jnp.dot(
             lt_ref[pl.ds(r0, NB), :], rt_ref[...], preferred_element_type=F32
         )
-        base = lax.div(r0, 128)
-        half = r[:, :128]
-        for h in range(1, parts):
-            half = jnp.where(base == h, r[:, 128 * h : 128 * h + 128], half)
-        d = pltpu.roll(half, lax.rem(128 - (r0 - base * 128), 128), 1)
-        catch_up(a_ref, lt_ref, rt_ref, q_ref, b)
-
-        inside = (lane >= r0) & (lane < r0 + NB)
-        rz = jnp.where(inside, 0.0, r)
-        start = jnp.where(inside, jnp.where(lane - r0 == row, -1.0, 0.0), r)
-        x = [
-            [d[8 * m : 8 * m + 8]] + [start[8 * m : 8 * m + 8, 128 * h : 128 * h + 128] for h in range(parts)]
-            for m in range(groups)
-        ]
-        for p in range(0, NB, 2):
-            i, s = p // 8, p % 8
-            left = [every(x[m][0][:, p : p + 1]) for m in range(groups)]
-            right = [every(x[m][0][:, p + 1 : p + 2]) for m in range(groups)]
-            a, c, e = every(left[i][s : s + 1]), every(right[i][s : s + 1]), every(right[i][s + 1 : s + 2])
-            det = a * e - c * c
-            inv = pl.reciprocal(det, approx=True)
-            inv = inv * (2.0 - det * inv)
-            inv = inv * (2.0 - det * inv)
-            fa, fc, fe = a * inv, c * inv, e * inv
-            for v in range(parts + 1):
-                yp, yq = every(x[i][v][s : s + 1]), every(x[i][v][s + 1 : s + 2])
-                wp = fe * yp - fc * yq
-                wq = fa * yq - fc * yp
-                for m in range(groups):
-                    x[m][v] = x[m][v] - left[m] * wp - right[m] * wq
-                x[i][v] = jnp.where(row8 == s, wp, jnp.where(row8 == s + 1, wq, x[i][v]))
-        q = jnp.concatenate([jnp.concatenate(x[m][1:], axis=1) for m in range(groups)], axis=0)
-        r1, r2, r3 = split3(rz)
+        catch_up(a_ref, lt_ref, rt_ref, q_ref, r0)
+        r1, r2, r3 = split3(jnp.where((lane >= r0) & (lane < r0 + NB), 0.0, r))
+        lt_ref[...] = jnp.concatenate([r1, r1, r2, r2, r1, r3], axis=0).T
+        half = [r[:, 128 * v : 128 * v + 128] for v in range(parts)]
+        own = half[0]
+        for v in range(1, parts):
+            own = jnp.where(h == v, half[v], own)
+        half = [own] + [jnp.where(h == v, half[0], half[v]) for v in range(1, parts)]
+        x = [[y[8 * m : 8 * m + 8] for y in half] for m in range(groups)]
+        for u in range(NB // SUB):
+            mine = range(u * wide, (u + 1) * wide)
+            rest = [m for m in range(groups) if m not in mine]
+            first = l0 + u * SUB
+            spread = lambda m, j: jnp.broadcast_to(x[m][0][:, first + j : first + j + 1], (8, 128))
+            cols = [{m: spread(m, j) for m in mine} for j in range(SUB)]
+            left = {m: [spread(m, j) for j in range(SUB)] for m in rest}
+            slot = 0
+
+            def rows_of(y, s):
+                nonlocal slot
+                tmp_ref[slot] = y
+                found = [jnp.broadcast_to(tmp_ref[slot, i : i + 1, :], (8, 128)) for i in (s, s + 1)]
+                slot += 1
+                return found
+
+            for p in range(0, SUB, 2):
+                i, s = u * wide + p // 8, p % 8
+                a, c = rows_of(cols[p][i], s)
+                _, e = rows_of(cols[p + 1][i], s)
+                det = a * e - c * c
+                inv = pl.reciprocal(det, approx=True)
+                inv = inv * (2.0 - det * inv)
+                inv = inv * (2.0 - det * inv)
+
+                def apply(y):
+                    yp, yq = rows_of(y[i], s)
+                    np_ = e * yp - c * yq
+                    nq_ = a * yq - c * yp
+                    done = {m: y[m] - (cols[p][m] * np_ + cols[p + 1][m] * nq_) * inv for m in mine}
+                    done[i] = jnp.where(row8 == s, np_ * inv, jnp.where(row8 == s + 1, nq_ * inv, done[i]))
+                    return done
+
+                for j in range(p + 2, SUB):
+                    cols[j] = apply(cols[j])
+                here = (lane8 == first + p) | (lane8 == first + p + 1)
+                unit = jnp.where(lane8 - first - p == row8 - s, -1.0, 0.0)
+                for m in mine:
+                    x[m][0] = jnp.where(here, unit if m == i else 0.0, x[m][0])
+                for v in range(parts):
+                    done = apply({m: x[m][v] for m in mine})
+                    for m in mine:
+                        x[m][v] = done[m]
+            ours = (lane8 >= first) & (lane8 < first + SUB)
+            base = slot
+            for m in mine:
+                for v in range(parts):
+                    tmp_ref[slot] = x[m][v]
+                    slot += 1
+            for m in rest:
+                x[m][0] = jnp.where(ours, 0.0, x[m][0])
+                for v in range(parts):
+                    terms = [
+                        left[m][j] * jnp.broadcast_to(tmp_ref[base + j // 8 * parts + v, j % 8 : j % 8 + 1, :], (8, 128))
+                        for j in range(SUB)
+                    ]
+                    while len(terms) > 1:
+                        terms = [terms[k] + terms[k + 1] for k in range(0, len(terms), 2)]
+                    x[m][v] = x[m][v] - terms[0]
+        half = [jnp.concatenate([x[m][v] for m in range(groups)], axis=0) for v in range(parts)]
+        half = [jnp.where(h == 0, half[0], half[1]), jnp.where(h == 0, half[1], half[0])]
+        q = jnp.concatenate(half, axis=1)
         q1, q2, q3 = split3(q)
-        lt_ref[...] = jnp.concatenate([r1, r1, r2, r2, r1, r3], axis=0).T
         rt_ref[...] = jnp.concatenate([q1, q2, q1, q2, q3, q1], axis=0)
         q_ref[...] = q
-        return carry
-
-    lax.fori_loop(first, last, panel, 0)
-
-
-def catch_up(a_ref, lt_ref, rt_ref, q_ref, b):
+
+
+def catch_up(a_ref, lt_ref, rt_ref, q_ref, r0):
     rank = a_ref.shape[0]
-    r0 = b * NB
     lane = lax.broadcasted_iota(jnp.int32, (rank, rank), 1)
     update = jnp.dot(lt_ref[...], rt_ref[...], preferred_element_type=F32)
     a_ref[...] = jnp.where((lane >= r0 - NB) & (lane < r0), 0.0, a_ref[...]) - update
     a_ref[pl.ds(pl.multiple_of(jnp.maximum(r0 - NB, 0), NB), NB), :] = q_ref[...]
 
 
-def sweep_begin(a_ref, lt_ref, rt_ref, q_ref):
+def sweep_begin(a_ref, lt_ref, rt_ref, q_ref, tmp_ref):
     lt_ref[...] = jnp.zeros_like(lt_ref)
     rt_ref[...] = jnp.zeros_like(rt_ref)
     q_ref[...] = a_ref[:NB, :]
 
 
-def sweep_end(a_ref, lt_ref, rt_ref, q_ref):
-    catch_up(a_ref, lt_ref, rt_ref, q_ref, a_ref.shape[0] // NB)
+def sweep_end(a_ref, lt_ref, rt_ref, q_ref, tmp_ref):
+    catch_up(a_ref, lt_ref, rt_ref, q_ref, a_ref.shape[0])
 
 
 def diagonal(matrix):
@@ -131,7 +162,7 @@
     n_x, n_z, total_a, total_b,
     t_hbm, b_hbm, c_hbm,
     hat_a_hbm, w_a_hbm, hat_b_hbm, w_b_hbm,
-    hat_a_ref, w_a_ref, hat_b_ref, w_b_ref, b_ref, c_ref, t_f32, t_hi, t_lo, bz, bfull, bst, call, pb, pbc, hs, pby, gb, gc, ma, ra, pa, pg, gz, gs, ga, sysm, lt, rt, qp, scl, iw,
+    hat_a_ref, w_a_ref, hat_b_ref, w_b_ref, b_ref, c_ref, t_f32, t_hi, t_lo, bz, bfull, bst, call, pb, pbc, hs, pby, gb, gc, ma, ra, pa, pg, gz, gs, ga, sysm, lt, rt, qp, tmp, scl, iw,
     mbt, mb, rb1, mb1, rb2, sq, sqp, sqs, sqz,
     t_sem, out_sem, send_sem, recv_sem,
 ):
@@ -267,9 +298,14 @@
     arrived(6, gb.at[0])
 
     scl[...] = scale_system(sysm, gb[...].reshape(rank, rank) * gc[...])
-    sweep = (sysm, lt, rt, qp)
+    sweep = (sysm, lt, rt, qp, tmp)
+
+    def half_of(h, carry):
+        sweep_half(*sweep, h)
+        return carry
+
     sweep_begin(*sweep)
-    sweep_panels(*sweep, 0, rank // NB)
+    lax.fori_loop(0, rank // 128, half_of, 0)
     sweep_end(*sweep)
     arrived(5, ra.at[pl.ds(0, n_s - 1)])
     share_a = jnp.sum(ra[...], axis=0)
@@ -324,14 +360,21 @@
         result.start()
     down = 1.0 / jnp.sqrt(down * (1.0 / total_a) + epsilon)
     scl[...] = scale_system(sysm, gram * down * iw[...] * gc[...])
-    middle = rank // NB // 2
     sweep_begin(*sweep)
-    sweep_panels(*sweep, 0, middle)
-    arrived(10, rb1.at[pl.ds(0, n_g - 1)])
-    mb1[...] = jnp.sum(rb1[...], axis=0)
-    fan(11, n_z, z_peer, lambda where: mb1.at[where], rb2.at[z])
-    rb2[z] = mb1[z]
-    sweep_panels(*sweep, middle, rank // NB)
+
+    def half_with_sums(h, carry):
+        sweep_half(*sweep, h)
+
+        @pl.when(h == 0)
+        def _():
+            arrived(10, rb1.at[pl.ds(0, n_g - 1)])
+            mb1[...] = jnp.sum(rb1[...], axis=0)
+            fan(11, n_z, z_peer, lambda where: mb1.at[where], rb2.at[z])
+            rb2[z] = mb1[z]
+
+        return carry
+
+    lax.fori_loop(0, rank // 128, half_with_sums, 0)
     sweep_end(*sweep)
     arrived(11, rb2.at[pl.ds(0, n_z - 1)])
     share_b = jnp.sum(rb2[...], axis=0)
@@ -425,6 +468,7 @@
             v((rank, 6 * NB), BF16),
             v((6 * NB, rank), BF16),
             v((NB, rank), F32),
+            v((128, 8, 128), F32),
             v((1, rank), F32),
             v((1, rank), F32),
             v((rank, width), F32),

time: 106 us -> 80.6 us (0.76)
  Pallas kernels: 106 us -> 79.9 us
    pallas_call x1, Pallas kernels: 104 us -> 78.2 us  [local(): pl.pallas_call(functools.partial(kernel, n_x, n_z, height * lax.axis_size...]
where the time goes in v4:
time: 80.6 us; the launch traced here: 80.5 us
  Pallas kernels  79.9 us (99%)
    pallas_call x1, Pallas kernels, local(): pl.pallas_call(functools.partial(kernel, n_x, n_z, height * lax.axis_size...  78.2 us
    pallas_call x1, Pallas kernels, local(): pl.pallas_call(finish, out_shape=results, in_specs=[hbm] * 4, out_specs=[...  1.7 us

profile of v4, /device:TPU:1, one launch (start us, length us, event | category | flops | bytes accessed | tf_op | source)
XLA Modules:
  0.0 80.5 jit_solution(15240663771973755019)
XLA Ops:
  0.6 78.2 %shard_map.66 = (f32[8,256]{1,0:T(8,128)}, f32[1,256]{1,0:T(1,128)}, f32[8,256]{1,0:T(8,128)}, f32[1,256]{1,0:T(1,128)}) custom-call(f32[24,128,512]{2,1,0:T(8,128)} %t_hbm.1, f32[8,256]{1,0:T(8,128)} %b_hbm.1, f32[24,256]{1,0:T(8,128)} %c_hbm.1), custom_call_target="tpu_custom_call" | custom-call | tf_op jit(solution)/shard_map/pallas_call | solution.py:435
  78.8 1.7 %shard_map.67 = (f32[8,256]{1,0:T(8,128)}, f32[1,256]{1,0:T(1,128)}, f32[8,256]{1,0:T(8,128)}, f32[1,256]{1,0:T(1,128)}) custom-call(f32[8,256]{1,0:T(8,128)} %get-tuple-element.12.refs_0_, f32[1,256]{1,0:T(1,128)} %get-tuple-element.13.refs_1_, f32[8,256]{1,0:T(8,128)} %get-tuple-element.14.refs_2_, f32[1,256]{1,0:T(1,128)} %get-tuple-element.15.refs_3_), custom_call_target="tpu_custom_call" | custom-call | tf_op jit(solution)/shard_map/pallas_call | solution.py:492

commit v5 on v4

--- a/solution.py
+++ b/solution.py
@@ -65,40 +65,62 @@
             left = {m: [spread(m, j) for j in range(SUB)] for m in rest}
             slot = 0
 
-            def rows_of(y, s):
+            def keep(y):
                 nonlocal slot
                 tmp_ref[slot] = y
-                found = [jnp.broadcast_to(tmp_ref[slot, i : i + 1, :], (8, 128)) for i in (s, s + 1)]
                 slot += 1
-                return found
-
+                return slot - 1
+
+            def row_of(where, s):
+                return jnp.broadcast_to(tmp_ref[where, s : s + 1, :], (8, 128))
+
+            kept = [{mine[0]: keep(cols[j][mine[0]])} for j in range(SUB)]
+            a, c, e = row_of(kept[0][mine[0]], 0), row_of(kept[0][mine[0]], 1), row_of(kept[1][mine[0]], 1)
             for p in range(0, SUB, 2):
                 i, s = u * wide + p // 8, p % 8
-                a, c = rows_of(cols[p][i], s)
-                _, e = rows_of(cols[p + 1][i], s)
+                i2, s2 = u * wide + (p + 2) // 8, (p + 2) % 8
                 det = a * e - c * c
-                inv = pl.reciprocal(det, approx=True)
-                inv = inv * (2.0 - det * inv)
-                inv = inv * (2.0 - det * inv)
-
-                def apply(y):
-                    yp, yq = rows_of(y[i], s)
-                    np_ = e * yp - c * yq
-                    nq_ = a * yq - c * yp
+                guess = pl.reciprocal(det, approx=True)
+                off = 1.0 - det * guess
+                inv = (guess + guess * off) * (1.0 + off * off)
+
+                def combine(yp, yq):
+                    return e * yp - c * yq, a * yq - c * yp
+
+                def apply(y, np_, nq_):
                     done = {m: y[m] - (cols[p][m] * np_ + cols[p + 1][m] * nq_) * inv for m in mine}
-                    done[i] = jnp.where(row8 == s, np_ * inv, jnp.where(row8 == s + 1, nq_ * inv, done[i]))
-                    return done
-
+                    plain = done[i]
+                    done[i] = jnp.where(row8 == s, np_ * inv, jnp.where(row8 == s + 1, nq_ * inv, plain))
+                    return done, plain
+
+                mixed = {j: combine(row_of(kept[j][i], s), row_of(kept[j][i], s + 1)) for j in range(p + 2, SUB)}
+                if p + 2 < SUB:
+                    for j in range(p, p + 4):
+                        if i2 not in kept[j]:
+                            kept[j][i2] = keep(cols[j][i2])
+                    (lp0, lp1), (lq0, lq1) = [[row_of(kept[j][i2], s2 + k) for k in (0, 1)] for j in (p, p + 1)]
+                    a0, c0 = row_of(kept[p + 2][i2], s2), row_of(kept[p + 2][i2], s2 + 1)
+                    e0 = row_of(kept[p + 3][i2], s2 + 1)
+                    (np2, nq2), (np3, nq3) = mixed[p + 2], mixed[p + 3]
+                    following = (
+                        a0 - (lp0 * np2 + lq0 * nq2) * inv,
+                        c0 - (lp1 * np2 + lq1 * nq2) * inv,
+                        e0 - (lp1 * np3 + lq1 * nq3) * inv,
+                    )
                 for j in range(p + 2, SUB):
-                    cols[j] = apply(cols[j])
+                    cols[j], plain = apply(cols[j], *mixed[j])
+                    kept[j] = {i2: keep(plain if i2 == i else cols[j][i2])}
                 here = (lane8 == first + p) | (lane8 == first + p + 1)
                 unit = jnp.where(lane8 - first - p == row8 - s, -1.0, 0.0)
                 for m in mine:
                     x[m][0] = jnp.where(here, unit if m == i else 0.0, x[m][0])
                 for v in range(parts):
-                    done = apply({m: x[m][v] for m in mine})
+                    where = keep(x[i][v])
+                    done, _ = apply({m: x[m][v] for m in mine}, *combine(row_of(where, s), row_of(where, s + 1)))
                     for m in mine:
                         x[m][v] = done[m]
+                if p + 2 < SUB:
+                    a, c, e = following
             ours = (lane8 >= first) & (lane8 < first + SUB)
             base = slot
             for m in mine:
@@ -148,21 +170,22 @@
     return jnp.sum(kept, axis=0, keepdims=True), jnp.sum(kept, axis=1, keepdims=True)
 
 
-def scale_system(a_ref, product):
-    rank = product.shape[0]
+def set_system(a_ref, gram, along, down, gc, gc_along, gc_down):
+    rank = gram.shape[0]
     eye = lax.broadcasted_iota(jnp.int32, (rank, rank), 0) == lax.broadcasted_iota(jnp.int32, (rank, rank), 1)
-    system = product + jnp.where(eye, ridge_term, 0.0)
-    along, down = diagonal(system)
-    along, down = lax.rsqrt(along), lax.rsqrt(down)
-    a_ref[...] = system * down * along
-    return along
+    (g_along, f_along), (g_down, f_down) = along, down
+    s_along = lax.rsqrt(g_along * f_along * f_along * gc_along + ridge_term)
+    s_down = lax.rsqrt(g_down * f_down * f_down * gc_down + ridge_term)
+    scaled = gram * (f_down * s_down) * (f_along * s_along) * gc
+    a_ref[...] = scaled + jnp.where(eye, ridge_term * s_along * s_along, 0.0)
+    return s_along
 
 
 def kernel(
     n_x, n_z, total_a, total_b,
     t_hbm, b_hbm, c_hbm,
     hat_a_hbm, w_a_hbm, hat_b_hbm, w_b_hbm,
-    hat_a_ref, w_a_ref, hat_b_ref, w_b_ref, b_ref, c_ref, t_f32, t_hi, t_lo, bz, bfull, bst, call, pb, pbc, hs, pby, gb, gc, ma, ra, pa, pg, gz, gs, ga, sysm, lt, rt, qp, tmp, scl, iw,
+    hat_a_ref, w_a_ref, hat_b_ref, w_b_ref, b_ref, c_ref, t_f32, t_hi, t_lo, bfull, bst, call, pb, pbc, hs, pby, gb, gc, gca, gcd, ma, ra, pa, pg, gz, gs, ga, sysm, lt, rt, qp, tmp, scl, iw,
     mbt, mb, rb1, mb1, rb2, sq, sqp, sqs, sqz,
     t_sem, out_sem, send_sem, recv_sem,
 ):
@@ -238,9 +261,11 @@
 
     for load in small:
         load.wait()
-    fan(0, n_z, z_peer, lambda _: b_ref, bz.at[z])
+    for d in range(1, n_z):
+        send(14 + d, b_ref, bfull.at[z, g], z_peer(d)[1])
+    fan(2, n_g, group_peer, lambda _: b_ref, bfull.at[z, g])
     fan(1, n_x, x_peer, lambda _: c_ref, call.at[ka])
-    bz[z] = b_ref[...]
+    bfull[z, g] = b_ref[...]
     call[ka] = c_ref[...]
 
     def cut(first, last):
@@ -252,10 +277,10 @@
 
         lax.fori_loop(first, last, body, 0)
 
-    early = n_chunk // 2
-    arrived(0, bz.at[pl.ds(0, n_z - 1)])
-    fan(2, n_g, group_peer, lambda _: bz, bfull.at[:, g])
-    bfull[:, g] = bz[...]
+    for d in sorted(range(1, n_z), key=lambda d: min(d, n_z - d)):
+        block = bfull.at[zs[n_z - d], g]
+        arrived(14 + d, block)
+        fan(2, n_g, group_peer, lambda _: block, block)
     for i in range(n_chunk):
         loads[i].wait()
         cut(i * per, (i + 1) * per)
@@ -263,6 +288,7 @@
         arrived(1, call.at[pl.ds(0, n_x - 1)])
     call_rows = call[...].reshape(n_x * depth, rank)
     gc[...] = lax.dot_general(call_rows, call_rows, TN, precision=HIGH, preferred_element_type=F32)
+    gca[...], gcd[...] = diagonal(gc[...])
 
     arrived(2, bfull.at[:, pl.ds(0, n_g - 1)])
     rows_b = bfull[...].reshape(width, rank)
@@ -285,19 +311,22 @@
         ma[...] = total.reshape(ma.shape)
         return carry
 
-    lax.fori_loop(0, early, first_mode, 0)
+    lax.fori_loop(0, 1, first_mode, 0)
     arrived(3, pbc)
     hs[...] = pb[core] + pbc[...]
     send(4, hs, pby, across)
-    lax.fori_loop(early, n_chunk, first_mode, 0)
-    fan(5, n_s, share_peer, lambda where: ma.at[where], ra.at[s])
-    ra[s] = ma[s]
+    lax.fori_loop(1, n_chunk - 1, first_mode, 0)
     arrived(4, pby)
     gb[core] = hs[...] + pby[...]
     send(6, gb.at[core], gb.at[core], sibling)
+    lax.fori_loop(n_chunk - 1, n_chunk, first_mode, 0)
+    fan(5, n_s, share_peer, lambda where: ma.at[where], ra.at[s])
+    ra[s] = ma[s]
     arrived(6, gb.at[0])
 
-    scl[...] = scale_system(sysm, gb[...].reshape(rank, rank) * gc[...])
+    gram_b = gb[...].reshape(rank, rank)
+    along, down = diagonal(gram_b)
+    scl[...] = set_system(sysm, gram_b, (along, 1.0), (down, 1.0), gc[...], gca[...], gcd[...])
     sweep = (sysm, lt, rt, qp, tmp)
 
     def half_of(h, carry):
@@ -333,12 +362,12 @@
         )
         return carry
 
-    lax.fori_loop(0, early, second_mode, 0)
+    lax.fori_loop(0, 2, second_mode, 0)
     arrived(8, gz.at[pl.ds(0, n_z - 1)])
     gs[...] = jnp.sum(gz[...], axis=0)
     fan(9, n_q, plane_peer, lambda _: gs, ga.at[q])
     ga[q] = gs[...]
-    lax.fori_loop(early, n_chunk, second_mode, 0)
+    lax.fori_loop(2, n_chunk, second_mode, 0)
     mb[...] = mbt[...].T.reshape(mb.shape)
     fan(10, n_g, group_peer, lambda where: mb.at[:, where], rb1.at[g])
     rb1[g] = mb[:, g]
@@ -358,8 +387,8 @@
     ]
     for result in results[:2]:
         result.start()
-    down = 1.0 / jnp.sqrt(down * (1.0 / total_a) + epsilon)
-    scl[...] = scale_system(sysm, gram * down * iw[...] * gc[...])
+    iw_down = 1.0 / jnp.sqrt(down * (1.0 / total_a) + epsilon)
+    scl[...] = set_system(sysm, gram, (along, iw[...]), (down, iw_down), gc[...], gca[...], gcd[...])
     sweep_begin(*sweep)
 
     def half_with_sums(h, carry):
@@ -394,7 +423,8 @@
     for result in results[2:]:
         result.start()
 
-    sent(0, bz.at[pl.ds(0, n_z - 1)])
+    for d in range(1, n_z):
+        sent(14 + d, bfull.at[z, g])
     if n_x > 1:
         sent(1, call.at[pl.ds(0, n_x - 1)])
     sent(2, bfull.at[:, pl.ds(0, n_g - 1)])
@@ -447,7 +477,6 @@
             v((depth, height, width), F32),
             v((depth, height, width), BF16),
             v((depth, height, width), BF16),
-            v((n_z, 8, rank), F32),
             v((n_z, n_g, 8, rank), F32),
             v((3 * width, rank), BF16),
             v((n_x, depth, rank), F32),
@@ -457,6 +486,8 @@
             v((rank // 2, rank), F32),
             v((2, rank // 2, rank), F32),
             v((rank, rank), F32),
+            v((1, rank), F32),
+            v((rank, 1), F32),
             v((n_s, 8, rank), F32),
             v((n_s, 8, rank), F32),
             v((n_q, 8, rank), F32),
@@ -468,7 +499,7 @@
             v((rank, 6 * NB), BF16),
             v((6 * NB, rank), BF16),
             v((NB, rank), F32),
-            v((128, 8, 128), F32),
+            v((160, 8, 128), F32),
             v((1, rank), F32),
             v((1, rank), F32),
             v((rank, width), F32),
@@ -482,8 +513,8 @@
             v((n_z, 1, rank), F32),
             pltpu.SemaphoreType.DMA((n_chunk + 2,)),
             pltpu.SemaphoreType.DMA((4,)),
-            pltpu.SemaphoreType.DMA((14,)),
-            pltpu.SemaphoreType.DMA((14,)),
+            pltpu.SemaphoreType.DMA((14 + n_z,)),
+            pltpu.SemaphoreType.DMA((14 + n_z,)),
         ],
         compiler_params=pltpu.CompilerParams(
             collective_id=0, has_side_effects=True, vmem_limit_bytes=VMEM_LIMIT

time: 80.6 us -> 78.3 us (0.971)
  Pallas kernels: 79.9 us -> 77.6 us
    pallas_call x1, Pallas kernels: 78.2 us -> 75.9 us  [local(): pl.pallas_call(functools.partial(kernel, n_x, n_z, height * lax.axis_size...]
where the time goes in v5:
time: 78.3 us
  Pallas kernels  77.6 us (99%)
    pallas_call x1, Pallas kernels, local(): pl.pallas_call(functools.partial(kernel, n_x, n_z, height * lax.axis_size...  75.9 us
    pallas_call x1, Pallas kernels, local(): pl.pallas_call(finish, out_shape=results, in_specs=[hbm] * 4, out_specs=[...  1.7 us

profile of v5, /device:TPU:1, one launch (start us, length us, event | category | flops | bytes accessed | tf_op | source)
XLA Modules:
  0.0 78.3 jit_solution(16229083507079363473)
XLA Ops:
  0.6 75.9 %shard_map.66 = (f32[8,256]{1,0:T(8,128)}, f32[1,256]{1,0:T(1,128)}, f32[8,256]{1,0:T(8,128)}, f32[1,256]{1,0:T(1,128)}) custom-call(f32[24,128,512]{2,1,0:T(8,128)} %t_hbm.1, f32[8,256]{1,0:T(8,128)} %b_hbm.1, f32[24,256]{1,0:T(8,128)} %c_hbm.1), custom_call_target="tpu_custom_call" | custom-call | tf_op jit(solution)/shard_map/pallas_call | solution.py:465
  76.6 1.7 %shard_map.67 = (f32[8,256]{1,0:T(8,128)}, f32[1,256]{1,0:T(1,128)}, f32[8,256]{1,0:T(8,128)}, f32[1,256]{1,0:T(1,128)}) custom-call(f32[8,256]{1,0:T(8,128)} %get-tuple-element.12.refs_0_, f32[1,256]{1,0:T(1,128)} %get-tuple-element.13.refs_1_, f32[8,256]{1,0:T(8,128)} %get-tuple-element.14.refs_2_, f32[1,256]{1,0:T(1,128)} %get-tuple-element.15.refs_3_), custom_call_target="tpu_custom_call" | custom-call | tf_op jit(solution)/shard_map/pallas_call | solution.py:523

commit v6 on v5

--- a/solution.py
+++ b/solution.py
@@ -49,7 +49,6 @@
         )
         catch_up(a_ref, lt_ref, rt_ref, q_ref, r0)
         r1, r2, r3 = split3(jnp.where((lane >= r0) & (lane < r0 + NB), 0.0, r))
-        lt_ref[...] = jnp.concatenate([r1, r1, r2, r2, r1, r3], axis=0).T
         half = [r[:, 128 * v : 128 * v + 128] for v in range(parts)]
         own = half[0]
         for v in range(1, parts):
@@ -127,6 +126,8 @@
                 for v in range(parts):
                     tmp_ref[slot] = x[m][v]
                     slot += 1
+            if u == 0:
+                lt_ref[...] = jnp.concatenate([r1, r1, r2, r2, r1, r3], axis=0).T
             for m in rest:
                 x[m][0] = jnp.where(ours, 0.0, x[m][0])
                 for v in range(parts):
@@ -147,9 +148,11 @@
 
 def catch_up(a_ref, lt_ref, rt_ref, q_ref, r0):
     rank = a_ref.shape[0]
-    lane = lax.broadcasted_iota(jnp.int32, (rank, rank), 1)
+    lane = lax.broadcasted_iota(jnp.int32, (8, rank), 1)
+    done = (lane >= r0 - NB) & (lane < r0)
     update = jnp.dot(lt_ref[...], rt_ref[...], preferred_element_type=F32)
-    a_ref[...] = jnp.where((lane >= r0 - NB) & (lane < r0), 0.0, a_ref[...]) - update
+    rest = jnp.where(done[None], 0.0, a_ref[...].reshape(rank // 8, 8, rank))
+    a_ref[...] = rest.reshape(rank, rank) - update
     a_ref[pl.ds(pl.multiple_of(jnp.maximum(r0 - NB, 0), NB), NB), :] = q_ref[...]
 
 
@@ -186,7 +189,7 @@
     t_hbm, b_hbm, c_hbm,
     hat_a_hbm, w_a_hbm, hat_b_hbm, w_b_hbm,
     hat_a_ref, w_a_ref, hat_b_ref, w_b_ref, b_ref, c_ref, t_f32, t_hi, t_lo, bfull, bst, call, pb, pbc, hs, pby, gb, gc, gca, gcd, ma, ra, pa, pg, gz, gs, ga, sysm, lt, rt, qp, tmp, scl, iw,
-    mbt, mb, rb1, mb1, rb2, sq, sqp, sqs, sqz,
+    at, ctb, mbt, mb, rb1, mb1, rb2, sq, sqp, sqs, sqz,
     t_sem, out_sem, send_sem, recv_sem,
 ):
     depth, height, width = t_f32.shape
@@ -268,6 +271,10 @@
     bfull[z, g] = b_ref[...]
     call[ka] = c_ref[...]
 
+    ct = jnp.concatenate([c_ref[...], jnp.zeros((128 - depth, rank), F32)], axis=0).T
+    for k in range(depth):
+        ctb[k] = jnp.broadcast_to(ct[:, k : k + 1], (rank, height))
+
     def cut(first, last):
         def body(k, carry):
             hi, lo = split2(t_f32[k])
@@ -292,7 +299,10 @@
 
     arrived(2, bfull.at[:, pl.ds(0, n_g - 1)])
     rows_b = bfull[...].reshape(width, rank)
-    pb[...] = lax.dot_general(rows_b, rows_b, TN, precision=HIGH, preferred_element_type=F32).reshape(pb.shape)
+    side = rank // 2
+    upper = lax.dot_general(rows_b[:, :side], rows_b, TN, precision=HIGH, preferred_element_type=F32)
+    corner = lax.dot_general(rows_b[:, side:], rows_b[:, side:], TN, precision=HIGH, preferred_element_type=F32)
+    pb[...] = jnp.concatenate([upper[:, :side], upper[:, side:], corner], axis=0).reshape(pb.shape)
     sibling = (ia, ja + 1 - 2 * core, ka)
     across = (z * 2 + 1 - yl, ja + 2 - 4 * yh, ka)
     send(3, pb.at[1 - core], pbc, sibling)
@@ -324,7 +334,14 @@
     ra[s] = ma[s]
     arrived(6, gb.at[0])
 
-    gram_b = gb[...].reshape(rank, rank)
+    blocks = gb[...].reshape(3 * side, side)
+    gram_b = jnp.concatenate(
+        [
+            jnp.concatenate([blocks[:side], blocks[side : 2 * side]], axis=1),
+            jnp.concatenate([blocks[side : 2 * side].T, blocks[2 * side :]], axis=1),
+        ],
+        axis=0,
+    )
     along, down = diagonal(gram_b)
     scl[...] = set_system(sysm, gram_b, (along, 1.0), (down, 1.0), gc[...], gca[...], gcd[...])
     sweep = (sysm, lt, rt, qp, tmp)
@@ -349,16 +366,15 @@
     gz[z] = pg[q]
     mbt[...] = jnp.zeros_like(mbt)
 
+    at[...] = pa[pl.ds(yl * n_s, n_s)].reshape(height, rank).T
+
     def second_mode(i, carry):
         k0 = i * per
-        rows = pa[pl.ds(yl * n_s, n_s)].reshape(height, rank)
-        both = jnp.concatenate([rows * c_ref[pl.ds(k0 + j, 1), :] for j in range(per)], axis=0)
-        hi, lo = split2(both)
+        hi, lo = zip(*[split2(at[...] * ctb[k0 + j]) for j in range(per)])
         th = t_hi[pl.ds(k0, per)].reshape(per * height, width)
         tl = t_lo[pl.ds(k0, per)].reshape(per * height, width)
-        mbt[...] += lax.dot_general(
-            jnp.concatenate([hi, lo, hi], axis=0), jnp.concatenate([th, th, tl], axis=0), TN,
-            preferred_element_type=F32,
+        mbt[...] += jnp.dot(
+            jnp.concatenate(hi + lo + hi, axis=1), jnp.concatenate([th, th, tl], axis=0), preferred_element_type=F32
         )
         return carry
 
@@ -480,11 +496,11 @@
             v((n_z, n_g, 8, rank), F32),
             v((3 * width, rank), BF16),
             v((n_x, depth, rank), F32),
-            v((2, rank // 2, rank), F32),
-            v((rank // 2, rank), F32),
-            v((rank // 2, rank), F32),
-            v((rank // 2, rank), F32),
-            v((2, rank // 2, rank), F32),
+            v((2, 3 * rank // 4, rank // 2), F32),
+            v((3 * rank // 4, rank // 2), F32),
+            v((3 * rank // 4, rank // 2), F32),
+            v((3 * rank // 4, rank // 2), F32),
+            v((2, 3 * rank // 4, rank // 2), F32),
             v((rank, rank), F32),
             v((1, rank), F32),
             v((rank, 1), F32),
@@ -502,6 +518,8 @@
             v((160, 8, 128), F32),
             v((1, rank), F32),
             v((1, rank), F32),
+            v((rank, height), F32),
+            v((depth, rank, height), F32),
             v((rank, width), F32),
             v((n_z, n_g, 8, rank), F32),
             v((n_g, n_z, 8, rank), F32),

time: 78.3 us -> 77.4 us (0.989)
  Pallas kernels: 77.6 us -> 76.7 us
    pallas_call x1, Pallas kernels: 75.9 us -> 75 us  [local(): pl.pallas_call(functools.partial(kernel, n_x, n_z, height * lax.axis_size...]
where the time goes in v6:
time: 77.4 us; the launch traced here: 77.3 us
  Pallas kernels  76.7 us (99%)
    pallas_call x1, Pallas kernels, local(): pl.pallas_call(functools.partial(kernel, n_x, n_z, height * lax.axis_size...  75 us
    pallas_call x1, Pallas kernels, local(): pl.pallas_call(finish, out_shape=results, in_specs=[hbm] * 4, out_specs=[...  1.7 us

profile of v6, /device:TPU:1, one launch (start us, length us, event | category | flops | bytes accessed | tf_op | source)
XLA Modules:
  0.0 77.3 jit_solution(17776303357931672144)
XLA Ops:
  0.6 75.0 %shard_map.66 = (f32[8,256]{1,0:T(8,128)}, f32[1,256]{1,0:T(1,128)}, f32[8,256]{1,0:T(8,128)}, f32[1,256]{1,0:T(1,128)}) custom-call(f32[24,128,512]{2,1,0:T(8,128)} %t_hbm.1, f32[8,256]{1,0:T(8,128)} %b_hbm.1, f32[24,256]{1,0:T(8,128)} %c_hbm.1), custom_call_target="tpu_custom_call" | custom-call | tf_op jit(solution)/shard_map/pallas_call | solution.py:481
  75.6 1.7 %shard_map.67 = (f32[8,256]{1,0:T(8,128)}, f32[1,256]{1,0:T(1,128)}, f32[8,256]{1,0:T(8,128)}, f32[1,256]{1,0:T(1,128)}) custom-call(f32[8,256]{1,0:T(8,128)} %get-tuple-element.12.refs_0_, f32[1,256]{1,0:T(1,128)} %get-tuple-element.13.refs_1_, f32[8,256]{1,0:T(8,128)} %get-tuple-element.14.refs_2_, f32[1,256]{1,0:T(1,128)} %get-tuple-element.15.refs_3_), custom_call_target="tpu_custom_call" | custom-call | tf_op jit(solution)/shard_map/pallas_call | solution.py:541

commit v7 on v6

--- a/solution.py
+++ b/solution.py
@@ -188,8 +188,8 @@
     n_x, n_z, total_a, total_b,
     t_hbm, b_hbm, c_hbm,
     hat_a_hbm, w_a_hbm, hat_b_hbm, w_b_hbm,
-    hat_a_ref, w_a_ref, hat_b_ref, w_b_ref, b_ref, c_ref, t_f32, t_hi, t_lo, bfull, bst, call, pb, pbc, hs, pby, gb, gc, gca, gcd, ma, ra, pa, pg, gz, gs, ga, sysm, lt, rt, qp, tmp, scl, iw,
-    at, ctb, mbt, mb, rb1, mb1, rb2, sq, sqp, sqs, sqz,
+    hat_a_ref, w_a_ref, hat_b_ref, w_b_ref, b_ref, c_ref, t_f32, t_hi, t_lo, bfull, bst, call, pb, pbc, hs, pby, gb, gc, gca, gcd, ma, ra, pa, pg, gz, ga, sysm, lt, rt, qp, tmp, scl, iw,
+    at, ctb, mbt, mb, rb1, mb1, rb2, sqp, sqz,
     t_sem, out_sem, send_sem, recv_sem,
 ):
     depth, height, width = t_f32.shape
@@ -199,9 +199,10 @@
     yh, core = lax.div(ja, 2), lax.rem(ja, 2)
     n_s = 4 * n_x
     n_q = 2 * n_s
+    n_p = n_s
     n_g = 2 * n_x
     s = ja * n_x + ka
-    q = yl * n_s + s
+    q = core * n_p + (yl * 2 + yh) * n_x + ka
     g = yl * n_x + ka
 
     yls = [lax.rem(yl + d, 2) for d in range(2)]
@@ -211,8 +212,8 @@
     ias = [z * 2 + yl2 for yl2 in yls]
 
     def plane_peer(d):
-        y, j, k = d // n_s, d // n_x % 4, d % n_x
-        return yls[y] * n_s + jas[j] * n_x + kas[k], (ias[y], jas[j], kas[k])
+        y, j, k = d // (2 * n_x), d // n_x % 2, d % n_x
+        return None, (ias[y], jas[2 * j], kas[k])
 
     def group_peer(d):
         y, k = d // n_x, d % n_x
@@ -224,6 +225,10 @@
 
     def z_peer(d):
         return zs[d], (zs[d] * 2 + yl, ja, ka)
+
+    def line_peer(d):
+        c, k = d // n_z, d % n_z
+        return None, (zs[k] * 2 + yl, ja + c * (1 - 2 * core), ka)
 
     def x_peer(d):
         return kas[d], (ia, ja, kas[d])
@@ -244,6 +249,17 @@
 
     def sent(stage, ref):
         pltpu.make_async_copy(ref, ref, send_sem.at[stage]).wait()
+
+    sibling = (ia, ja + 1 - 2 * core, ka)
+    across = (z * 2 + 1 - yl, ja + 2 - 4 * yh, ka)
+
+    def over_chips(stage, buf):
+        fan(stage, n_p, plane_peer, lambda _: buf.at[q], buf.at[q])
+
+    def over_cores(stage, forward, buf):
+        arrived(stage, buf.at[pl.ds(0, n_p - 1)])
+        ours = buf.at[pl.ds(core * n_p, n_p)]
+        send(forward, ours, ours, sibling)
 
     n_chunk = t_sem.shape[0] - 2
     per = depth // n_chunk
@@ -257,16 +273,16 @@
 
     barrier = pltpu.get_barrier_semaphore()
 
-    for count, peer in ((n_z, z_peer), (n_q, plane_peer)):
-        for d in range(1, count):
-            pl.semaphore_signal(barrier, inc=1, device_id=peer(d)[1], device_id_type=MESH)
-    pl.semaphore_wait(barrier, n_q + n_z - 2)
+    greeted = [line_peer(d) for d in range(1, 2 * n_z) if d != n_z] + [plane_peer(d) for d in range(1, n_p)]
+    greeted += [share_peer(d) for d in range(n_s) if d // n_x % 2]
+    for _, device in greeted:
+        pl.semaphore_signal(barrier, inc=1, device_id=device, device_id_type=MESH)
+    pl.semaphore_wait(barrier, len(greeted))
 
     for load in small:
         load.wait()
     for d in range(1, n_z):
         send(14 + d, b_ref, bfull.at[z, g], z_peer(d)[1])
-    fan(2, n_g, group_peer, lambda _: b_ref, bfull.at[z, g])
     fan(1, n_x, x_peer, lambda _: c_ref, call.at[ka])
     bfull[z, g] = b_ref[...]
     call[ka] = c_ref[...]
@@ -284,10 +300,9 @@
 
         lax.fori_loop(first, last, body, 0)
 
-    for d in sorted(range(1, n_z), key=lambda d: min(d, n_z - d)):
-        block = bfull.at[zs[n_z - d], g]
-        arrived(14 + d, block)
-        fan(2, n_g, group_peer, lambda _: block, block)
+    for d in range(1, n_z):
+        arrived(14 + d, bfull.at[zs[n_z - d], g])
+    fan(2, n_g, group_peer, lambda _: bfull.at[:, g], bfull.at[:, g])
     for i in range(n_chunk):
         loads[i].wait()
         cut(i * per, (i + 1) * per)
@@ -303,8 +318,6 @@
     upper = lax.dot_general(rows_b[:, :side], rows_b, TN, precision=HIGH, preferred_element_type=F32)
     corner = lax.dot_general(rows_b[:, side:], rows_b[:, side:], TN, precision=HIGH, preferred_element_type=F32)
     pb[...] = jnp.concatenate([upper[:, :side], upper[:, side:], corner], axis=0).reshape(pb.shape)
-    sibling = (ia, ja + 1 - 2 * core, ka)
-    across = (z * 2 + 1 - yl, ja + 2 - 4 * yh, ka)
     send(3, pb.at[1 - core], pbc, sibling)
     hi, lo = split2(rows_b)
     bst[...] = jnp.concatenate([hi, lo, hi], axis=0)
@@ -358,15 +371,19 @@
     raw_a = -jnp.dot(share_a * scl[...], sysm[...], precision=HIGH, preferred_element_type=F32) * scl[...]
 
     pa[q] = raw_a
-    fan(7, n_q, plane_peer, lambda _: pa.at[q], pa.at[q])
-    arrived(7, pa.at[pl.ds(0, n_q - 1)])
+    over_chips(7, pa)
+    over_cores(7, 0, pa)
+    arrived(0, pa.at[pl.ds(0, n_p)])
     rows_a = pa[...].reshape(n_q * 8, rank)
     pg[...] = lax.dot_general(rows_a, rows_a, TN, precision=HIGH, preferred_element_type=F32).reshape(pg.shape)
     fan(8, n_z, z_peer, lambda _: pg.at[q], gz.at[z])
     gz[z] = pg[q]
     mbt[...] = jnp.zeros_like(mbt)
 
-    at[...] = pa[pl.ds(yl * n_s, n_s)].reshape(height, rank).T
+    ours = [
+        pa[pl.ds(c * n_p + (yl * 2 + y) * n_x, n_x)].reshape(n_x * 8, rank) for y in range(2) for c in range(2)
+    ]
+    at[...] = jnp.concatenate(ours, axis=0).T
 
     def second_mode(i, carry):
         k0 = i * per
@@ -380,15 +397,16 @@
 
     lax.fori_loop(0, 2, second_mode, 0)
     arrived(8, gz.at[pl.ds(0, n_z - 1)])
-    gs[...] = jnp.sum(gz[...], axis=0)
-    fan(9, n_q, plane_peer, lambda _: gs, ga.at[q])
-    ga[q] = gs[...]
-    lax.fori_loop(2, n_chunk, second_mode, 0)
+    ga[q] = jnp.sum(gz[...], axis=0)
+    over_chips(9, ga)
+    lax.fori_loop(2, n_chunk - 1, second_mode, 0)
+    over_cores(9, 14, ga)
+    lax.fori_loop(n_chunk - 1, n_chunk, second_mode, 0)
     mb[...] = mbt[...].T.reshape(mb.shape)
     fan(10, n_g, group_peer, lambda where: mb.at[:, where], rb1.at[g])
     rb1[g] = mb[:, g]
 
-    arrived(9, ga.at[pl.ds(0, n_q - 1)])
+    arrived(14, ga.at[pl.ds(0, n_p)])
     gram = ga[...].reshape(rank, rank)
     along, down = diagonal(gram)
     weight_a = jnp.sqrt(along * (1.0 / total_a) + epsilon)
@@ -425,14 +443,14 @@
     share_b = jnp.sum(rb2[...], axis=0)
     raw_b = -jnp.dot(share_b * iw[...] * scl[...], sysm[...], precision=HIGH, preferred_element_type=F32) * scl[...]
 
-    sq[...] = jnp.sum(raw_b * raw_b, axis=0, keepdims=True)
-    fan(12, n_q, plane_peer, lambda _: sq, sqp.at[q])
-    sqp[q] = sq[...]
-    arrived(12, sqp.at[pl.ds(0, n_q - 1)])
-    sqs[...] = jnp.sum(sqp[...], axis=0)
-    fan(13, n_z, z_peer, lambda _: sqs, sqz.at[z])
-    sqz[z] = sqs[...]
-    arrived(13, sqz.at[pl.ds(0, n_z - 1)])
+    mine = yl * 2 * n_x + yh * n_x + ka
+    sqp[mine] = jnp.sum(raw_b * raw_b, axis=0, keepdims=True)
+    fan(12, n_p, plane_peer, lambda _: sqp.at[mine], sqp.at[mine])
+    arrived(12, sqp.at[pl.ds(0, n_p - 1)])
+    line = core * n_z + z
+    sqz[line] = jnp.sum(sqp[...], axis=0)
+    fan(13, 2 * n_z, line_peer, lambda _: sqz.at[line], sqz.at[line])
+    arrived(13, sqz.at[pl.ds(0, 2 * n_z - 1)])
     weight_b = jnp.sqrt(jnp.sum(sqz[...], axis=0) * (1.0 / total_b) + epsilon)
     w_b_ref[...] = weight_b
     hat_b_ref[...] = raw_b / weight_b
@@ -448,13 +466,15 @@
     sent(4, pby)
     sent(5, ra.at[pl.ds(0, n_s - 1)])
     sent(6, gb.at[0])
-    sent(7, pa.at[pl.ds(0, n_q - 1)])
+    sent(7, pa.at[pl.ds(0, n_p - 1)])
+    sent(0, pa.at[pl.ds(0, n_p)])
     sent(8, gz.at[pl.ds(0, n_z - 1)])
-    sent(9, ga.at[pl.ds(0, n_q - 1)])
+    sent(9, ga.at[pl.ds(0, n_p - 1)])
+    sent(14, ga.at[pl.ds(0, n_p)])
     sent(10, rb1.at[pl.ds(0, n_g - 1)])
     sent(11, rb2.at[pl.ds(0, n_z - 1)])
-    sent(12, sqp.at[pl.ds(0, n_q - 1)])
-    sent(13, sqz.at[pl.ds(0, n_z - 1)])
+    sent(12, sqp.at[pl.ds(0, n_p - 1)])
+    sent(13, sqz.at[pl.ds(0, 2 * n_z - 1)])
     for result in results:
         result.wait()
 
@@ -509,7 +529,6 @@
             v((n_q, 8, rank), F32),
             v((n_q, part, rank), F32),
             v((n_z, part, rank), F32),
-            v((part, rank), F32),
             v((n_q, part, rank), F32),
             v((rank, rank), F32),
             v((rank, 6 * NB), BF16),
@@ -525,10 +544,8 @@
             v((n_g, n_z, 8, rank), F32),
             v((n_z, 8, rank), F32),
             v((n_z, 8, rank), F32),
-            v((1, rank), F32),
-            v((n_q, 1, rank), F32),
-            v((1, rank), F32),
-            v((n_z, 1, rank), F32),
+            v((n_s, 1, rank), F32),
+            v((2 * n_z, 1, rank), F32),
             pltpu.SemaphoreType.DMA((n_chunk + 2,)),
             pltpu.SemaphoreType.DMA((4,)),
             pltpu.SemaphoreType.DMA((14 + n_z,)),

time: 77.4 us -> 84.7 us (1.094)
  Pallas kernels: 76.7 us -> 84 us
    pallas_call x1, Pallas kernels: 75 us -> 82.3 us  [local(): pl.pallas_call(functools.partial(kernel, n_x, n_z, height * lax.axis_size...]
where the time goes in v7:
time: 84.7 us; the launch traced here: 84.6 us
  Pallas kernels  84 us (99%)
    pallas_call x1, Pallas kernels, local(): pl.pallas_call(functools.partial(kernel, n_x, n_z, height * lax.axis_size...  82.3 us
    pallas_call x1, Pallas kernels, local(): pl.pallas_call(finish, out_shape=results, in_specs=[hbm] * 4, out_specs=[...  1.7 us

profile of v7, /device:TPU:1, one launch (start us, length us, event | category | flops | bytes accessed | tf_op | source)
XLA Modules:
  0.0 84.6 jit_solution(5250392241889528597)
XLA Ops:
  0.6 82.3 %shard_map.66 = (f32[8,256]{1,0:T(8,128)}, f32[1,256]{1,0:T(1,128)}, f32[8,256]{1,0:T(8,128)}, f32[1,256]{1,0:T(1,128)}) custom-call(f32[24,128,512]{2,1,0:T(8,128)} %t_hbm.1, f32[8,256]{1,0:T(8,128)} %b_hbm.1, f32[24,256]{1,0:T(8,128)} %c_hbm.1), custom_call_target="tpu_custom_call" | custom-call | tf_op jit(solution)/shard_map/pallas_call | solution.py:501
  82.9 1.7 %shard_map.67 = (f32[8,256]{1,0:T(8,128)}, f32[1,256]{1,0:T(1,128)}, f32[8,256]{1,0:T(8,128)}, f32[1,256]{1,0:T(1,128)}) custom-call(f32[8,256]{1,0:T(8,128)} %get-tuple-element.12.refs_0_, f32[1,256]{1,0:T(1,128)} %get-tuple-element.13.refs_1_, f32[8,256]{1,0:T(8,128)} %get-tuple-element.14.refs_2_, f32[1,256]{1,0:T(1,128)} %get-tuple-element.15.refs_3_), custom_call_target="tpu_custom_call" | custom-call | tf_op jit(solution)/shard_map/pallas_call | solution.py:558

commit v8 on v6

--- a/solution.py
+++ b/solution.py
@@ -32,7 +32,7 @@
     return hi, mid, (rest - mid.astype(F32)).astype(BF16)
 
 
-def sweep_half(a_ref, lt_ref, rt_ref, q_ref, tmp_ref, h):
+def sweep_half(a_ref, lt_ref, rt_ref, q_ref, tmp_ref, h, between=None):
     rank = a_ref.shape[0]
     parts = rank // 128
     row8 = lax.broadcasted_iota(jnp.int32, (8, 128), 0)
@@ -41,6 +41,8 @@
     groups = NB // 8
     wide = SUB // 8
     for t in range(128 // NB):
+        if between is not None and t == 2:
+            pl.when(h == rank // 128 - 1)(between)
         l0 = t * NB
         r0 = pl.multiple_of(h * 128 + l0, NB)
         before = (lane >= r0 - NB) & (lane < r0)
@@ -87,9 +89,10 @@
                     return e * yp - c * yq, a * yq - c * yp
 
                 def apply(y, np_, nq_):
-                    done = {m: y[m] - (cols[p][m] * np_ + cols[p + 1][m] * nq_) * inv for m in mine}
+                    wp, wq = np_ * inv, nq_ * inv
+                    done = {m: y[m] - cols[p][m] * wp - cols[p + 1][m] * wq for m in mine}
                     plain = done[i]
-                    done[i] = jnp.where(row8 == s, np_ * inv, jnp.where(row8 == s + 1, nq_ * inv, plain))
+                    done[i] = jnp.where(row8 == s, wp, jnp.where(row8 == s + 1, wq, plain))
                     return done, plain
 
                 mixed = {j: combine(row_of(kept[j][i], s), row_of(kept[j][i], s + 1)) for j in range(p + 2, SUB)}
@@ -188,7 +191,7 @@
     n_x, n_z, total_a, total_b,
     t_hbm, b_hbm, c_hbm,
     hat_a_hbm, w_a_hbm, hat_b_hbm, w_b_hbm,
-    hat_a_ref, w_a_ref, hat_b_ref, w_b_ref, b_ref, c_ref, t_f32, t_hi, t_lo, bfull, bst, call, pb, pbc, hs, pby, gb, gc, gca, gcd, ma, ra, pa, pg, gz, gs, ga, sysm, lt, rt, qp, tmp, scl, iw,
+    hat_a_ref, w_a_ref, hat_b_ref, w_b_ref, b_ref, c_ref, t_f32, t_hi, t_lo, bfull, bst, call, pb, pbc, hs, pby, gb, gc, gca, gcd, ma, ra, pa, at2, gz, gs, ga, sysm, lt, rt, qp, tmp, scl, iw,
     at, ctb, mbt, mb, rb1, mb1, rb2, sq, sqp, sqs, sqz,
     t_sem, out_sem, send_sem, recv_sem,
 ):
@@ -361,9 +364,10 @@
     fan(7, n_q, plane_peer, lambda _: pa.at[q], pa.at[q])
     arrived(7, pa.at[pl.ds(0, n_q - 1)])
     rows_a = pa[...].reshape(n_q * 8, rank)
-    pg[...] = lax.dot_general(rows_a, rows_a, TN, precision=HIGH, preferred_element_type=F32).reshape(pg.shape)
-    fan(8, n_z, z_peer, lambda _: pg.at[q], gz.at[z])
-    gz[z] = pg[q]
+    part = gz.shape[1]
+    at2[...] = rows_a.T
+    gz[z] = jnp.dot(at2[pl.ds(pl.multiple_of(q * part, part), part), :], rows_a, precision=HIGH, preferred_element_type=F32)
+    fan(8, n_z, z_peer, lambda _: gz.at[z], gz.at[z])
     mbt[...] = jnp.zeros_like(mbt)
 
     at[...] = pa[pl.ds(yl * n_s, n_s)].reshape(height, rank).T
@@ -378,12 +382,12 @@
         )
         return carry
 
-    lax.fori_loop(0, 2, second_mode, 0)
+    lax.fori_loop(0, n_chunk // 2, second_mode, 0)
     arrived(8, gz.at[pl.ds(0, n_z - 1)])
     gs[...] = jnp.sum(gz[...], axis=0)
     fan(9, n_q, plane_peer, lambda _: gs, ga.at[q])
     ga[q] = gs[...]
-    lax.fori_loop(2, n_chunk, second_mode, 0)
+    lax.fori_loop(n_chunk // 2, n_chunk, second_mode, 0)
     mb[...] = mbt[...].T.reshape(mb.shape)
     fan(10, n_g, group_peer, lambda where: mb.at[:, where], rb1.at[g])
     rb1[g] = mb[:, g]
@@ -407,16 +411,14 @@
     scl[...] = set_system(sysm, gram, (along, iw[...]), (down, iw_down), gc[...], gca[...], gcd[...])
     sweep_begin(*sweep)
 
+    def pass_sums():
+        arrived(10, rb1.at[pl.ds(0, n_g - 1)])
+        mb1[...] = jnp.sum(rb1[...], axis=0)
+        fan(11, n_z, z_peer, lambda where: mb1.at[where], rb2.at[z])
+        rb2[z] = mb1[z]
+
     def half_with_sums(h, carry):
-        sweep_half(*sweep, h)
-
-        @pl.when(h == 0)
-        def _():
-            arrived(10, rb1.at[pl.ds(0, n_g - 1)])
-            mb1[...] = jnp.sum(rb1[...], axis=0)
-            fan(11, n_z, z_peer, lambda where: mb1.at[where], rb2.at[z])
-            rb2[z] = mb1[z]
-
+        sweep_half(*sweep, h, pass_sums)
         return carry
 
     lax.fori_loop(0, rank // 128, half_with_sums, 0)
@@ -507,7 +509,7 @@
             v((n_s, 8, rank), F32),
             v((n_s, 8, rank), F32),
             v((n_q, 8, rank), F32),
-            v((n_q, part, rank), F32),
+            v((rank, n_q * 8), F32),
             v((n_z, part, rank), F32),
             v((part, rank), F32),
             v((n_q, part, rank), F32),

time: 77.4 us -> 78.3 us (1.012)
  Pallas kernels: 76.7 us -> 77.6 us
    pallas_call x1, Pallas kernels: 75 us -> 75.9 us  [local(): pl.pallas_call(functools.partial(kernel, n_x, n_z, height * lax.axis_size...]
where the time goes in v8:
time: 78.3 us; the launch traced here: 78.2 us
  Pallas kernels  77.6 us (99%)
    pallas_call x1, Pallas kernels, local(): pl.pallas_call(functools.partial(kernel, n_x, n_z, height * lax.axis_size...  75.9 us
    pallas_call x1, Pallas kernels, local(): pl.pallas_call(finish, out_shape=results, in_specs=[hbm] * 4, out_specs=[...  1.7 us

profile of v8, /device:TPU:1, one launch (start us, length us, event | category | flops | bytes accessed | tf_op | source)
XLA Modules:
  0.0 78.2 jit_solution(15760982072575496242)
XLA Ops:
  0.6 75.9 %shard_map.66 = (f32[8,256]{1,0:T(8,128)}, f32[1,256]{1,0:T(1,128)}, f32[8,256]{1,0:T(8,128)}, f32[1,256]{1,0:T(1,128)}) custom-call(f32[24,128,512]{2,1,0:T(8,128)} %t_hbm.1, f32[8,256]{1,0:T(8,128)} %b_hbm.1, f32[24,256]{1,0:T(8,128)} %c_hbm.1), custom_call_target="tpu_custom_call" | custom-call | tf_op jit(solution)/shard_map/pallas_call | solution.py:483
  76.5 1.7 %shard_map.67 = (f32[8,256]{1,0:T(8,128)}, f32[1,256]{1,0:T(1,128)}, f32[8,256]{1,0:T(8,128)}, f32[1,256]{1,0:T(1,128)}) custom-call(f32[8,256]{1,0:T(8,128)} %get-tuple-element.12.refs_0_, f32[1,256]{1,0:T(1,128)} %get-tuple-element.13.refs_1_, f32[8,256]{1,0:T(8,128)} %get-tuple-element.14.refs_2_, f32[1,256]{1,0:T(1,128)} %get-tuple-element.15.refs_3_), custom_call_target="tpu_custom_call" | custom-call | tf_op jit(solution)/shard_map/pallas_call | solution.py:543

commit v9 on v8

--- a/solution.py
+++ b/solution.py
@@ -16,7 +16,7 @@
 BF16 = jnp.bfloat16
 VMEM_LIMIT = 65000000
 NB = 32
-SUB = 16
+SUB = 8
 TN = (((0,), (0,)), ((), ()))
 
 

time: 78.3 us -> 79.2 us (1.011)
  Pallas kernels: 77.6 us -> 78.5 us
    pallas_call x1, Pallas kernels: 75.9 us -> 76.8 us  [local(): pl.pallas_call(functools.partial(kernel, n_x, n_z, height * lax.axis_size...]
where the time goes in v9:
time: 79.2 us; the launch traced here: 79.1 us
  Pallas kernels  78.5 us (99%)
    pallas_call x1, Pallas kernels, local(): pl.pallas_call(functools.partial(kernel, n_x, n_z, height * lax.axis_size...  76.8 us
    pallas_call x1, Pallas kernels, local(): pl.pallas_call(finish, out_shape=results, in_specs=[hbm] * 4, out_specs=[...  1.7 us

profile of v9, /device:TPU:1, one launch (start us, length us, event | category | flops | bytes accessed | tf_op | source)
XLA Modules:
  0.0 79.1 jit_solution(1322880564950667812)
XLA Ops:
  0.6 76.8 %shard_map.66 = (f32[8,256]{1,0:T(8,128)}, f32[1,256]{1,0:T(1,128)}, f32[8,256]{1,0:T(8,128)}, f32[1,256]{1,0:T(1,128)}) custom-call(f32[24,128,512]{2,1,0:T(8,128)} %t_hbm.1, f32[8,256]{1,0:T(8,128)} %b_hbm.1, f32[24,256]{1,0:T(8,128)} %c_hbm.1), custom_call_target="tpu_custom_call" | custom-call | tf_op jit(solution)/shard_map/pallas_call | solution.py:483
  77.4 1.7 %shard_map.67 = (f32[8,256]{1,0:T(8,128)}, f32[1,256]{1,0:T(1,128)}, f32[8,256]{1,0:T(8,128)}, f32[1,256]{1,0:T(1,128)}) custom-call(f32[8,256]{1,0:T(8,128)} %get-tuple-element.12.refs_0_, f32[1,256]{1,0:T(1,128)} %get-tuple-element.13.refs_1_, f32[8,256]{1,0:T(8,128)} %get-tuple-element.14.refs_2_, f32[1,256]{1,0:T(1,128)} %get-tuple-element.15.refs_3_), custom_call_target="tpu_custom_call" | custom-call | tf_op jit(solution)/shard_map/pallas_call | solution.py:543
